TPU v7x, 32 devices: a whole 2x2x4 slice. The times are simulated.
32 devices in a mesh: dp: 4 (over y, x), mp: 8 (over z, core).
Axes of the slice: x: 2, y: 2, z: 4, core: 2. Of those that a mesh axis runs over, the one named last changes fastest.
Arguments:
- queries: bfloat16 [32, 48, 2048], P('dp'), may hold values from -3 to 3
- new_keys: bfloat16 [32, 48, 2048], P('dp'), may hold values from -3 to 3
- new_values: bfloat16 [32, 48, 2048], P('dp'), may hold values from -6 to 6
- cache_keys: bfloat16 [32, 1024, 2048], P('dp', 'mp'), may hold values from -3 to 3
- cache_values: bfloat16 [32, 1024, 2048], P('dp', 'mp'), may hold values from -6 to 6
- lengths: int32 [32], P('dp'), may hold values from 16 to 1024, as said below
- parents: int32 [32, 48], P('dp'), may hold values from 0 to 46, as said below
- tree_tokens: int32 [32, 48], P('dp'), may hold values from 0 to 19455
- residual: bfloat16 [32, 48, 2048], P('dp'), may hold values from -6 to 6
- out_weight: bfloat16 [2048, 2048], P(('dp', 'mp')), may hold values from -0.125 to 0.125
- norm_gain: float32 [2048], replicated, may hold values from 0.25 to 1.75
- vocab_weight: bfloat16 [2048, 19456], P(None, 'mp'), may hold values from -0.375 to 0.375
Outputs:
- hidden: bfloat16 [32, 48, 2048], P('dp')
- node_logprob: float32 [32, 48], P('dp')
Inputs may be any that keep to these rules, and one draw needn't show every extreme that they name: `lengths`: A request's cache length is 1024 or lies between 16 and 128; some request has length 1024 in every draw. parents[r, 0] is 0; for j > 0, parents[r, j] is j - 2 or j - 1 (0 for j = 1); some request's last node has parent 48 - 2 in every draw.
All inputs are finite; a program needn't handle non-finite values.
Results may differ from a plain program's by a relative error of at most 0.007.
Values may be sent and summed in bfloat16 or wider, within the bound.
A program may use at most 128 MiB of HBM per device.

v0:
```python
import jax
import jax.numpy as jnp
from jax import lax
from jax.sharding import PartitionSpec as P

HEADS = 16
SINK = 4


def ancestor_mask(parents):
    tree = parents.shape[-1]
    idx = jnp.arange(tree, dtype=jnp.int32)
    links = (
        (idx[None, :, None] == idx[None, None, :]) | (parents[:, :, None] == idx[None, None, :])
    ).astype(jnp.float32)
    for _ in range((tree - 1).bit_length()):
        links = jnp.minimum(
            jnp.einsum("rij,rjk->rik", links, links, precision=lax.Precision.HIGHEST), 1.0
        )
    return links > 0.5


def local(
    queries,
    new_keys,
    new_values,
    cache_keys,
    cache_values,
    lengths,
    parents,
    tree_tokens,
    residual,
    out_weight,
    norm_gain,
    vocab_weight,
):
    reqs, tree, width = queries.shape
    slots = cache_keys.shape[1]
    head_dim = width // HEADS
    scale = head_dim ** (-0.5)
    shard = lax.axis_index("mp")
    shards = lax.axis_size("mp")
    tokens = reqs * tree
    window = slots * shards // 2
    positions = shard * slots + jnp.arange(slots, dtype=jnp.int32)
    visible = (positions[None, :] < lengths[:, None]) & (
        (positions[None, :] < SINK) | (positions[None, :] >= lengths[:, None] - window)
    )
    q4 = queries.reshape(reqs, tree, HEADS, head_dim)
    k4 = cache_keys.reshape(reqs, slots, HEADS, head_dim)
    v4 = cache_values.reshape(reqs, slots, HEADS, head_dim)
    cache_e = jnp.where(
        visible[:, None, None, :],
        jnp.exp(jnp.einsum("rihd,rshd->rhis", q4, k4, preferred_element_type=jnp.float32) * scale),
        0.0,
    )
    cache_den = jnp.sum(cache_e, -1)
    cache_num = jnp.einsum(
        "rhis,rshd->rihd", cache_e.astype(jnp.bfloat16), v4, preferred_element_type=jnp.float32
    )
    ancestors = ancestor_mask(parents)
    nk4 = new_keys.reshape(reqs, tree, HEADS, head_dim)
    nv4 = new_values.reshape(reqs, tree, HEADS, head_dim)
    tree_e = jnp.where(
        ancestors[:, None],
        jnp.exp(jnp.einsum("rihd,rjhd->rhij", q4, nk4, preferred_element_type=jnp.float32) * scale),
        0.0,
    )
    tree_den = jnp.sum(tree_e, -1)
    tree_num = jnp.einsum(
        "rhij,rjhd->rihd", tree_e.astype(jnp.bfloat16), nv4, preferred_element_type=jnp.float32
    )
    flat_res = residual.reshape(tokens, width)
    num_all, den_all = lax.psum((cache_num.reshape(tokens, width), cache_den), "mp")
    denom = jnp.transpose(den_all + tree_den, (0, 2, 1))
    numer = num_all.reshape(reqs, tree, HEADS, head_dim) + tree_num
    attended = (numer / denom[..., None]).astype(jnp.bfloat16).reshape(tokens, width)
    projected = jnp.dot(
        attended,
        lax.all_gather(out_weight, ("dp", "mp"), axis=0, tiled=True),
        preferred_element_type=jnp.float32,
    )
    hidden = (flat_res.astype(jnp.float32) + projected).astype(jnp.bfloat16)
    hfloat = hidden.astype(jnp.float32)
    normed = (
        hfloat * lax.rsqrt(jnp.mean(hfloat * hfloat, -1, keepdims=True) + 1e-06) * norm_gain
    ).astype(jnp.bfloat16)
    vocab_dev = vocab_weight.shape[1]
    logits = jnp.dot(normed, vocab_weight, preferred_element_type=jnp.float32)
    exp_sums = jnp.sum(jnp.exp(logits), -1)
    parent_rows = (jnp.arange(reqs, dtype=jnp.int32)[:, None] * tree + parents).reshape(-1)
    column = tree_tokens.reshape(-1) - shard * vocab_dev
    inside = (column >= 0) & (column < vocab_dev)
    picked = jnp.where(inside, logits[parent_rows, jnp.clip(column, 0, vocab_dev - 1)], 0.0)
    parent_sums = exp_sums[parent_rows]
    total_sums, total_picked = lax.psum((parent_sums, picked), "mp")
    node_logprob = (total_picked - jnp.log(total_sums)).reshape(reqs, tree)
    return (hidden.reshape(reqs, tree, width), node_logprob)


def solution(mesh):
    placed = (
        P("dp", None, None),
        P("dp", None, None),
        P("dp", None, None),
        P("dp", "mp", None),
        P("dp", "mp", None),
        P("dp"),
        P("dp", None),
        P("dp", None),
        P("dp", None, None),
        P(("dp", "mp"), None),
        P(),
        P(None, "mp"),
    )
    return jax.shard_map(
        local,
        mesh=mesh,
        in_specs=placed,
        out_specs=(P("dp", None, None), P("dp", None)),
        check_vma=False,
    )
```

profile of v0, /device:TPU:0, one launch (start us, length us, event | category | flops | bytes accessed | tf_op | source)
XLA Modules:
  0.0 187.4 jit_solution(10211102734035660524)
XLA Ops:
  8.0 0.0 copy-start
  8.0 0.0 all-reduce.3.cloned.1.call-start
  8.1 0.8 broadcast_add_fusion.1
  8.9 0.7 or_and_fusion
  9.6 0.0 copy-done
  9.6 0.0 copy-start.1
  9.6 5.4 %fusion.12 = (f32[8,16,48]{2,1,0:T(8,128)S(1)}, f32[8,16,48,128]{3,2,1,0:T(8,128)S(1)}) fusion(pred[8,128]{1,0:T(8,128)(4,1)S(1)} %or_and_fusion, bf16[8,128,2048]{2,1,0:T(8,128)(2,1)} %param.15, bf16[8,48,2048]{2,1,0:T(8,128)(2,1)S(1)} %copy-done), kind=kOutput, calls=%fused_computation.21 | convolution fusion | flops 203679744 | bytes 8938496 | tf_op jit(solution)/shard_map/rihd,rshd->rhis/dot_general | solution.py:54
  15.0 0.0 copy-done.1
  15.1 3.0 %fusion.16 = f32[8,48,16,128]{3,1,2,0:T(8,128)} fusion(f32[8,16,48,128]{3,2,1,0:T(8,128)S(1)} %get-tuple-element.7, pred[8,128]{1,0:T(8,128)(4,1)S(1)} %or_and_fusion, bf16[8,128,2048]{2,1,0:T(8,128)(2,1)S(1)} %copy-done.1), kind=kOutput, calls=%fused_computation.25 | convolution fusion | flops 203685888 | bytes 10486784 | tf_op jit(solution)/shard_map/rhis,rshd->rihd/dot_general | solution.py:58
  18.0 0.0 copy-start.3
  18.0 0.0 copy-start.2
  18.0 0.0 copy-start.4
  18.1 0.0 all-reduce.3.cloned.1.call-update
  18.1 0.0 all-gather.2.cloned.1.call-start
  18.1 0.5 all-gather.2.cloned.1.call-update
  18.7 0.1 copy-done.3
  18.7 0.3 convolution_minimum_fusion.5
  19.0 0.3 convolution_minimum_fusion.4
  19.3 0.3 convolution_minimum_fusion.3
  19.7 0.3 convolution_minimum_fusion.2
  20.0 0.3 convolution_minimum_fusion.1
  20.3 0.3 fusion.42
  20.6 0.1 copy.25
  20.8 0.0 copy-done.2
  20.8 0.1 min.36
  20.9 0.1 broadcast_add_fusion
  21.0 0.1 reshape.212
  21.1 0.1 and.16
  21.2 32.3 %psum.29 = f32[8,16,48]{2,1,0:T(8,128)S(1)} all-reduce(f32[8,16,48]{2,1,0:T(8,128)S(1)} %get-tuple-element.6), channel_id=1, replica_groups=mesh['dp'=4,'mp'=8] {'mp'}, use_global_device_ids=true, to_apply=%region_2.3 | all-reduce | flops 6144 | bytes 49152 | tf_op jit(solution)/shard_map/psum | solution.py:74
  53.5 0.0 copy-done.4
  53.6 2.7 %fusion.14 = (f32[8,16,48]{2,1,0:T(8,128)S(1)}, f32[8,16,48,48]{2,3,1,0:T(8,128)}) fusion(pred[8,48,48]{1,2,0:T(8,128)(4,1)S(1)} %copy.25, bf16[8,48,2048]{2,1,0:T(8,128)(2,1)S(1)} %copy-done.4, bf16[8,48,2048]{2,1,0:T(8,128)(2,1)S(1)} %copy-done), kind=kOutput, calls=%fused_computation.23 | convolution fusion | flops 76376064 | bytes 4368384 | tf_op jit(solution)/shard_map/rihd,rjhd->rhij/dot_general | solution.py:66
  56.3 75.3 %all-reduce.3.cloned.1.call-done = f32[8,48,16,128]{3,1,2,0:T(8,128)} async-done(((f32[8,48,16,128]{3,1,2,0:T(8,128)}), f32[8,48,16,128]{3,1,2,0:T(8,128)}) %all-reduce.3.cloned.1.call-update) | async-done | bytes 3145744 | tf_op jit(solution)/shard_map/psum | solution.py:74
  131.5 4.9 %fusion.11 = bf16[8,48,16,128]{3,1,2,0:T(8,128)(2,1)S(1)} fusion(f32[8,48,16,128]{3,1,2,0:T(8,128)} %all-reduce.3.cloned.1.call-done, f32[8,16,48,48]{2,3,1,0:T(8,128)} %get-tuple-element.9, f32[8,48,16]{1,2,0:T(8,128)S(1)} %add_bitcast_fusion, pred[8,48,48]{1,2,0:T(8,128)(4,1)S(1)} %copy.25, bf16[8,48,2048]{2,1,0:T(8,128)(2,1)} %param.14), kind=kOutput, calls=%fused_computation.18 | convolution fusion | flops 78741504 | bytes 7514112 | tf_op jit(solution)/shard_map/rhij,rjhd->rihd/dot_general | solution.py:70
  136.5 0.4 copy.30
  136.9 0.0 all-gather.2.cloned.1.call-done
  136.9 0.0 copy-start.5
  136.9 7.4 %fusion.6 = (f32[384]{0:T(512)S(1)}, bf16[384,2048]{1,0:T(8,128)(2,1)S(1)}) fusion(bf16[2048,2048]{1,0:T(8,128)(2,1)} %all-gather.2.cloned.1.call-done, bf16[48,8,16,128]{3,2,1,0:T(8,128)(2,1)S(1)} %bitcast.82, bf16[384,2048]{1,0:T(8,128)(2,1)} %bitcast.83), kind=kOutput, calls=%fused_computation.11 | convolution fusion | flops 3225943552 | bytes 13108736 | tf_op jit(solution)/shard_map/dot_general | solution.py:78
  144.3 0.0 copy-start.6
  144.3 0.0 copy-done.5
  144.4 10.5 %exponential_reduce_fusion = (f32[384]{0:T(512)S(1)}, f32[384,2432]{1,0:T(8,128)}) fusion(bf16[2048,2432]{1,0:T(8,128)(2,1)} %param.23, bf16[384,2048]{1,0:T(8,128)(2,1)S(1)} %get-tuple-element.11, f32[2048]{0:T(1024)S(1)} %copy-done.5, f32[384]{0:T(512)S(1)} %add_rsqrt_fusion), kind=kOutput, calls=%fused_computation.10 | convolution fusion | flops 3829284352 | bytes 15281152 | tf_op jit(solution)/shard_map/dot_general | solution.py:89
  154.8 0.0 copy-done.6
  154.8 6.4 %gather_fusion = f32[384]{0:T(512)S(1)} fusion(f32[384,2432]{1,0:T(8,128)} %get-tuple-element.13, s32[384]{0:T(512)S(1)} %get-tuple-element.3), kind=kCustom, calls=%fused_computation | custom fusion | bytes 6144 | tf_op jit(solution)/shard_map/gather | solution.py:94
  161.2 2.8 %gather_fusion.1 = f32[384]{0:T(512)S(1)} fusion(f32[384]{0:T(512)S(1)} %get-tuple-element.12, s32[1024]{0:T(1024)S(1)} %pad_clamp_fusion), kind=kCustom, calls=%fused_computation.1 | custom fusion | bytes 4608 | tf_op jit(solution)/shard_map/gather | solution.py:95
  164.0 15.2 %all-reduce = (f32[384]{0:T(512)S(1)}, f32[384]{0:T(512)S(1)}) all-reduce(f32[384]{0:T(512)S(1)} %broadcast_select_fusion, f32[384]{0:T(512)S(1)} %gather_fusion.1), channel_id=1, replica_groups=mesh['dp'=4,'mp'=8] {'mp'}, use_global_device_ids=true, to_apply=%region_5.6 | all-reduce | flops 768 | bytes 6144 | tf_op jit(solution)/shard_map/psum | solution.py:96
  179.2 0.7 reshape.213
  (12 shorter events, 0.1 us)
Async XLA Ops:
  8.0 1.6 copy-start
  8.0 123.5 %all-reduce.3.cloned.1.call-start = ((), (), s32[]{:S(2)}) async-start(), calls=%async_computation | async-start | bytes 6291456 | tf_op jit(solution)/shard_map/psum | solution.py:74
  9.6 5.5 %copy-start.1 = (bf16[8,128,2048]{2,1,0:T(8,128)(2,1)S(1)}, bf16[8,128,2048]{2,1,0:T(8,128)(2,1)}, u32[]{:S(2)}) copy-start(bf16[8,128,2048]{2,1,0:T(8,128)(2,1)} %param.16) | copy-start | bytes 12582916
  18.0 0.7 copy-start.3
  18.0 2.8 %copy-start.2 = (s32[8,48]{1,0:T(8,128)S(1)}, s32[8,48]{1,0:T(8,128)}, u32[]{:S(2)}) copy-start(s32[8,48]{1,0:T(8,128)} %param.19) | copy-start | bytes 4612
  18.0 35.5 %copy-start.4 = (bf16[8,48,2048]{2,1,0:T(8,128)(2,1)S(1)}, bf16[8,48,2048]{2,1,0:T(8,128)(2,1)}, u32[]{:S(2)}) copy-start(bf16[8,48,2048]{2,1,0:T(8,128)(2,1)} %param.13) | copy-start | bytes 4718596
  18.1 118.8 %all-gather.2.cloned.1.call-start = ((), (), s32[]{:S(2)}) async-start(), calls=%async_computation.1 | async-start | bytes 8650752 | tf_op jit(solution)/shard_map/all_gather | solution.py:80
  136.9 7.4 %copy-start.5 = (f32[2048]{0:T(1024)S(1)}, f32[2048]{0:T(1024)}, u32[]{:S(2)}) copy-start(f32[2048]{0:T(1024)} %param.22) | copy-start | bytes 24580
  144.3 10.5 %copy-start.6 = (bf16[384,2048]{1,0:T(8,128)(2,1)}, bf16[384,2048]{1,0:T(8,128)(2,1)S(1)}, u32[]{:S(2)}) copy-start(bf16[384,2048]{1,0:T(8,128)(2,1)S(1)} %get-tuple-element.11) | copy-start | bytes 4718596
Sparse Core Ops, SparseCore 0:
  18.2 113.2 all-reduce.2
Sparse Core Ops, SparseCore 1:
  21.6 101.1 all-gather.1
where the time goes:
time: 188 us; the launch traced here: 187 us
  waiting for transfers between devices  75.8 us (40%)
  blocking collectives  47.5 us (25%)
  matrix products  35.8 us (19%)
  between operations  15.7 us (8%)
  local copies, waits for them, and re-layouts  10.7 us (6%)
    psum x1, waiting for transfers between devices, local(): lax.psum((cache_num.reshape(tokens, width), cache_den), 'mp')  75.3 us
    psum x1, blocking collectives, local(): lax.psum((cache_num.reshape(tokens, width), cache_den), 'mp')  32.3 us
    psum x1, blocking collectives, local(): total_sums, total_picked = lax.psum((parent_sums, picked), 'mp')  15.2 us
    dot_general x1, matrix products, local(): logits = jnp.dot(normed, vocab_weight, preferred_element_type=jnp.float32)  10.5 us
    dot_general x1, matrix products, local(): jnp.dot(attended, lax.all_gather(out_weight, ('dp', 'mp'), axis=0, tiled=...  7.39 us
    gather x1, local copies, waits for them, and re-layouts, local(): logits[parent_rows, jnp.clip(column, 0, vocab_dev - 1)]  6.37 us
    dot_general x1, matrix products, local(): jnp.einsum('rihd,rshd->rhis', q4, k4, preferred_element_type=jnp.float32)  5.44 us
    dot_general x1, matrix products, local(): jnp.einsum('rhij,rjhd->rihd', tree_e.astype(jnp.bfloat16), nv4, preferred...  4.93 us
  transfers between devices with their start and end apart: 2, of which 1 were waited for; matrix products, arithmetic and copies ran while one was open for 6% of the time, Pallas kernels for 0%

commit v1 on v0

--- a/solution.py
+++ b/solution.py
@@ -1,10 +1,18 @@
+import functools
+
 import jax
 import jax.numpy as jnp
 from jax import lax
+from jax.experimental import pallas as pl
+from jax.experimental.pallas import tpu as pltpu
 from jax.sharding import PartitionSpec as P
 
 HEADS = 16
 SINK = 4
+F32 = jnp.float32
+BF16 = jnp.bfloat16
+MESH = pl.DeviceIdType.MESH
+VMEM_LIMIT = 50 * 1024 * 1024
 
 
 def ancestor_mask(parents):
@@ -12,7 +20,7 @@
     idx = jnp.arange(tree, dtype=jnp.int32)
     links = (
         (idx[None, :, None] == idx[None, None, :]) | (parents[:, :, None] == idx[None, None, :])
-    ).astype(jnp.float32)
+    ).astype(F32)
     for _ in range((tree - 1).bit_length()):
         links = jnp.minimum(
             jnp.einsum("rij,rjk->rik", links, links, precision=lax.Precision.HIGHEST), 1.0
@@ -20,7 +28,445 @@
     return links > 0.5
 
 
-def local(
+def attention_kernel(shards, len_ref, q_ref, k_ref, v_ref, nk_ref, nv_ref, anc_ref, o_ref):
+    req = pl.program_id(0)
+    shard = lax.axis_index("mp")
+    slots = k_ref.shape[1]
+    tree, width = q_ref.shape[1:]
+    hd = width // HEADS
+    scale = hd ** (-0.5)
+    cap = slots * shards
+    length = len_ref[req]
+    start = shard * slots
+    tree_shard = max(shards // 8, 1)
+    seen = (start < length) & ((start < SINK) | (start + slots > length - cap // 2))
+
+    def attend(keys, values, mask):
+        lane = lax.broadcasted_iota(jnp.int32, (tree, 128), 1)
+        den = jnp.zeros((tree, 128), F32)
+        for h in range(HEADS):
+            cols = slice(h * hd, (h + 1) * hd)
+            s = lax.dot_general(
+                q_ref[0, :, cols], keys[0, :, cols], (((1,), (1,)), ((), ())),
+                preferred_element_type=F32,
+            )
+            e = jnp.where(mask, jnp.exp(s * scale), 0.0)
+            den = jnp.where(lane == h, jnp.sum(e, -1, keepdims=True), den)
+            o_ref[0, :, cols] = jnp.dot(
+                e.astype(BF16), values[0, :, cols], preferred_element_type=F32
+            ).astype(BF16)
+        o_ref[0, :, width:] = den.astype(BF16)
+
+    @pl.when(shard == tree_shard)
+    def _():
+        attend(nk_ref, nv_ref, anc_ref[0] > 0.5)
+
+    @pl.when((shard != tree_shard) & seen)
+    def _():
+        pos = start + lax.broadcasted_iota(jnp.int32, (tree, slots), 1)
+        attend(
+            k_ref, v_ref, (pos < length) & ((pos < SINK) | (pos >= length - cap // 2))
+        )
+
+    @pl.when((shard != tree_shard) & jnp.logical_not(seen))
+    def _():
+        o_ref[...] = jnp.zeros_like(o_ref)
+
+
+def attention(shards, queries, new_keys, new_values, cache_keys, cache_values, lengths, anc):
+    reqs, tree, width = queries.shape
+    slots = cache_keys.shape[1]
+
+    def block(rows, cols):
+        return pl.BlockSpec((1, rows, cols), lambda r: (r, 0, 0))
+
+    return pl.pallas_call(
+        functools.partial(attention_kernel, shards),
+        grid=(reqs,),
+        in_specs=[
+            pl.BlockSpec(memory_space=pltpu.SMEM),
+            block(tree, width),
+            block(slots, width),
+            block(slots, width),
+            block(tree, width),
+            block(tree, width),
+            block(tree, tree),
+        ],
+        out_specs=block(tree, width + 128),
+        out_shape=jax.ShapeDtypeStruct((reqs, tree, width + 128), BF16),
+        compiler_params=pltpu.CompilerParams(vmem_limit_bytes=VMEM_LIMIT),
+        name="attention_part",
+    )(lengths, queries, cache_keys, cache_values, new_keys, new_values, anc)
+
+
+def when(cond, fn):
+    pl.when(cond)(fn)
+
+
+def gather_line(chips, buf, recv, send_r, send_l, send_s):
+    me = lax.axis_index("mp")
+    c, z = lax.rem(me, 2), lax.div(me, 2)
+    sib = 2 * z + 1 - c
+
+    def copy(slot, sem, to):
+        return pltpu.make_async_remote_copy(
+            src_ref=buf.at[slot], dst_ref=buf.at[slot], send_sem=sem, recv_sem=recv.at[slot],
+            device_id={"mp": to}, device_id_type=MESH,
+        )
+
+    def right(k):
+        return copy(2 * (z - k) + c, send_r.at[k], me + 2)
+
+    def left(k):
+        return copy(2 * (z + k) + c, send_l.at[k], me - 2)
+
+    def pair(zs):
+        return copy(2 * zs + c, send_s.at[zs], sib)
+
+    when(z < chips - 1, lambda: right(0).start())
+    when(z > 0, lambda: left(0).start())
+    pair(z).start()
+    for k in range(1, chips):
+
+        @pl.when(z - k >= 0)
+        def _():
+            right(k).wait_recv()
+            when(z < chips - 1, lambda: right(k).start())
+            pair(z - k).start()
+
+        @pl.when(z + k <= chips - 1)
+        def _():
+            left(k).wait_recv()
+            when(z > 0, lambda: left(k).start())
+            pair(z + k).start()
+
+    for zs in range(chips):
+        copy(2 * zs + 1 - c, send_s.at[zs], sib).wait_recv()
+
+    def finish():
+        for k in range(chips):
+            when((z - k >= 0) & (z < chips - 1), lambda: right(k).wait_send())
+            when((z + k <= chips - 1) & (z > 0), lambda: left(k).wait_send())
+        for zs in range(chips):
+            pair(zs).wait_send()
+
+    return finish
+
+
+def hidden_kernel(
+    chips, groups, part, w_ref, res_ref, out_ref,
+    sib_buf, from_l, from_r, acc, tot, att, wcol, hcol,
+    sib_s, sib_r, fl_r, fr_r, acc_s, g1_r, g1_a, g1_b, g1_c, g2_r, g2_a, g2_b, g2_c,
+    w1_s, w1_r, w2_s, w2_r, own_s,
+):
+    shards = 2 * chips
+    me = lax.axis_index("mp")
+    grp = lax.axis_index("dp")
+    c, z = lax.rem(me, 2), lax.div(me, 2)
+    sib = 2 * z + 1 - c
+    width = att.shape[-1]
+    hd = width // HEADS
+    ncol = wcol.shape[-1]
+
+    barrier = pltpu.get_barrier_semaphore()
+    for k in range(1, shards):
+        pl.semaphore_signal(
+            barrier, inc=1, device_id={"mp": lax.rem(me + k, shards)}, device_id_type=MESH
+        )
+    for k in range(1, groups):
+        pl.semaphore_signal(
+            barrier, inc=1, device_id={"dp": lax.rem(grp + k, groups)}, device_id_type=MESH
+        )
+    pl.semaphore_wait(barrier, shards - 1 + groups - 1)
+
+    def pair(zd):
+        return pltpu.make_async_remote_copy(
+            src_ref=part.at[2 * zd + 1 - c], dst_ref=sib_buf.at[zd], send_sem=sib_s.at[zd],
+            recv_sem=sib_r.at[zd], device_id={"mp": sib}, device_id_type=MESH,
+        )
+
+    order = []
+    for k in range(chips):
+        for zd in (chips - 1 - k, k):
+            if zd not in order:
+                order.append(zd)
+    for zd in order:
+        pair(zd).start()
+
+    def columns(j):
+        return pl.ds(pl.multiple_of(j * ncol, 128), ncol)
+
+    def w_mp(k):
+        to = lax.rem(me + k, shards)
+        return pltpu.make_async_remote_copy(
+            src_ref=w_ref.at[:, columns(to)], dst_ref=wcol.at[grp, me], send_sem=w1_s.at[k],
+            recv_sem=w1_r.at[k], device_id={"mp": to}, device_id_type=MESH,
+        )
+
+    for k in range(1, shards):
+        w_mp(k).start()
+    own = pltpu.make_async_copy(w_ref.at[:, columns(me)], wcol.at[grp, me], own_s)
+    own.start()
+
+    def pass_on(zd, buf, sems, to):
+        return pltpu.make_async_remote_copy(
+            src_ref=acc.at[zd], dst_ref=buf.at[zd], send_sem=acc_s.at[zd],
+            recv_sem=sems.at[zd], device_id={"mp": to}, device_id_type=MESH,
+        )
+
+    def both(zd):
+        return part[2 * zd + c].astype(F32) + sib_buf[zd].astype(F32)
+
+    def step(zd, buf, sems, first, to):
+        pair(zd).wait_recv()
+
+        @pl.when(first)
+        def _():
+            acc[zd] = both(zd).astype(BF16)
+
+        @pl.when(jnp.logical_not(first))
+        def _():
+            pass_on(zd, buf, sems, to).wait_recv()
+            acc[zd] = (both(zd) + buf[zd].astype(F32)).astype(BF16)
+
+        pass_on(zd, buf, sems, to).start()
+
+    for k in range(chips - 1):
+        rd, ld = chips - 1 - k, k
+        when(rd > z, functools.partial(step, rd, from_l, fl_r, z == 0, me + 2))
+        when(ld < z, functools.partial(step, ld, from_r, fr_r, z == chips - 1, me - 2))
+
+    pair(z).wait_recv()
+    tot[...] = both(z)
+
+    @pl.when(z > 0)
+    def _():
+        pass_on(z, from_l, fl_r, me).wait_recv()
+        tot[...] += from_l[z].astype(F32)
+
+    @pl.when(z < chips - 1)
+    def _():
+        pass_on(z, from_r, fr_r, me).wait_recv()
+        tot[...] += from_r[z].astype(F32)
+
+    for h in range(HEADS):
+        cols = slice(h * hd, (h + 1) * hd)
+        att[me, :, cols] = (tot[:, cols] / tot[:, width + h : width + h + 1]).astype(BF16)
+
+    for k in range(1, shards):
+        w_mp(k).wait_recv()
+    own.wait()
+
+    def w_dp(k, src):
+        return pltpu.make_async_remote_copy(
+            src_ref=wcol.at[src], dst_ref=wcol.at[src], send_sem=w2_s.at[k],
+            recv_sem=w2_r.at[k], device_id={"dp": lax.rem(grp + k, groups)}, device_id_type=MESH,
+        )
+
+    for k in range(1, groups):
+        w_dp(k, grp).start()
+
+    done_1 = gather_line(chips, att, g1_r, g1_a, g1_b, g1_c)
+    for k in range(1, groups):
+        w_dp(k, lax.rem(grp + groups - k, groups)).wait_recv()
+
+    rows = att.shape[0] * att.shape[1]
+    projected = jnp.dot(
+        att[...].reshape(rows, width), wcol[...].reshape(width, ncol), preferred_element_type=F32
+    )
+    hcol[me] = (res_ref[...].astype(F32) + projected).astype(BF16)
+    done_2 = gather_line(chips, hcol, g2_r, g2_a, g2_b, g2_c)
+    for j in range(shards):
+        out_ref[:, j * ncol : (j + 1) * ncol] = hcol[j]
+
+    done_1()
+    done_2()
+    for zd in range(chips):
+        pair(zd).wait_send()
+        when(zd != z, lambda: pass_on(zd, from_l, fl_r, me).wait_send())
+    for k in range(1, shards):
+        w_mp(k).wait_send()
+    for k in range(1, groups):
+        w_dp(k, grp).wait_send()
+
+
+def hidden_of(shards, groups, part, out_weight, res):
+    own, width = part.shape[1], out_weight.shape[1]
+    wide = part.shape[2]
+    tokens = own * shards
+    ncol = width // shards
+    chips = shards // 2
+    dma = pltpu.SemaphoreType.DMA
+    gather_sems = [dma((shards,)), dma((chips,)), dma((chips,)), dma((chips,))]
+    vmem = pl.BlockSpec(memory_space=pltpu.VMEM)
+    return pl.pallas_call(
+        functools.partial(hidden_kernel, chips, groups),
+        in_specs=[vmem] * 3,
+        out_specs=vmem,
+        out_shape=jax.ShapeDtypeStruct((tokens, width), BF16),
+        scratch_shapes=[
+            pltpu.VMEM((chips, own, wide), BF16),
+            pltpu.VMEM((chips, own, wide), BF16),
+            pltpu.VMEM((chips, own, wide), BF16),
+            pltpu.VMEM((chips, own, wide), BF16),
+            pltpu.VMEM((own, wide), F32),
+            pltpu.VMEM((shards, own, width), BF16),
+            pltpu.VMEM((groups, shards, out_weight.shape[0], ncol), BF16),
+            pltpu.VMEM((shards, tokens, ncol), BF16),
+            dma((chips,)), dma((chips,)), dma((chips,)), dma((chips,)), dma((chips,)),
+            *gather_sems,
+            *gather_sems,
+            dma((shards,)), dma((shards,)), dma((groups,)), dma((groups,)), dma,
+        ],
+        compiler_params=pltpu.CompilerParams(
+            collective_id=0, has_side_effects=True, vmem_limit_bytes=VMEM_LIMIT
+        ),
+        name="hidden_exchange",
+    )(part, out_weight, res)
+
+
+def score_kernel(vocab, h_ref, g_ref, t_ref, w_ref, o_ref, normed, sums):
+    step = pl.program_id(0)
+    tile = w_ref.shape[1]
+    rows = h_ref.shape[0]
+
+    @pl.when(step == 0)
+    def _():
+        h = h_ref[...].astype(F32)
+        normed[...] = (
+            h * lax.rsqrt(jnp.mean(h * h, -1, keepdims=True) + 1e-06) * g_ref[...]
+        ).astype(BF16)
+        sums[...] = jnp.zeros_like(sums)
+
+    logits = jnp.dot(normed[...], w_ref[...], preferred_element_type=F32)
+    lane = lax.broadcasted_iota(jnp.int32, (rows, 128), 1)
+    marks = [t_ref[:, n : n + 1] for n in range(3)]
+    new = [jnp.zeros((rows, 128), F32) for _ in range(4)]
+    for b in range(tile // 128):
+        col = step * tile + b * 128 + lane
+        x = logits[:, b * 128 : (b + 1) * 128]
+        new[0] += jnp.where(col < vocab, jnp.exp(x), 0.0)
+        for n in range(3):
+            new[n + 1] += jnp.where(col == marks[n], x, 0.0)
+    for n in range(4):
+        sums[n] += new[n]
+
+    @pl.when(step == pl.num_programs(0) - 1)
+    def _():
+        stat = jnp.zeros((rows, 128), F32)
+        for n in range(4):
+            stat = jnp.where(lane == n, jnp.sum(sums[n], -1, keepdims=True), stat)
+        o_ref[...] = jnp.transpose(stat)[:8]
+
+
+def score(hidden, gain, marks, vocab_weight):
+    rows, width = hidden.shape
+    vocab = vocab_weight.shape[1]
+    tile = 512
+    return pl.pallas_call(
+        functools.partial(score_kernel, vocab),
+        grid=(pl.cdiv(vocab, tile),),
+        in_specs=[
+            pl.BlockSpec((rows, width), lambda i: (0, 0)),
+            pl.BlockSpec((1, width), lambda i: (0, 0)),
+            pl.BlockSpec((rows, 128), lambda i: (0, 0)),
+            pl.BlockSpec((width, tile), lambda i: (0, i)),
+        ],
+        out_specs=pl.BlockSpec((8, rows), lambda i: (0, 0)),
+        out_shape=jax.ShapeDtypeStruct((8, rows), F32),
+        scratch_shapes=[pltpu.VMEM((rows, width), BF16), pltpu.VMEM((4, rows, 128), F32)],
+        compiler_params=pltpu.CompilerParams(vmem_limit_bytes=VMEM_LIMIT),
+        name="score_part",
+    )(hidden, gain, marks, vocab_weight)
+
+
+def total_kernel(shards, x_ref, o_ref, slots, send, recv):
+    me = lax.axis_index("mp")
+    barrier = pltpu.get_barrier_semaphore()
+    for k in range(1, shards):
+        pl.semaphore_signal(
+            barrier, inc=1, device_id={"mp": lax.rem(me + k, shards)}, device_id_type=MESH
+        )
+    pl.semaphore_wait(barrier, shards - 1)
+
+    def copy(k):
+        return pltpu.make_async_remote_copy(
+            src_ref=x_ref, dst_ref=slots.at[k], send_sem=send.at[k], recv_sem=recv.at[k],
+            device_id={"mp": lax.rem(me + k, shards)}, device_id_type=MESH,
+        )
+
+    for k in range(1, shards):
+        copy(k).start()
+    total = x_ref[...]
+    for k in range(1, shards):
+        copy(k).wait_recv()
+        total = total + slots[k]
+    o_ref[...] = total
+    for k in range(1, shards):
+        copy(k).wait_send()
+
+
+def total_of(shards, stats):
+    vmem = pl.BlockSpec(memory_space=pltpu.VMEM)
+    dma = pltpu.SemaphoreType.DMA
+    return pl.pallas_call(
+        functools.partial(total_kernel, shards),
+        in_specs=[vmem],
+        out_specs=vmem,
+        out_shape=jax.ShapeDtypeStruct(stats.shape, F32),
+        scratch_shapes=[
+            pltpu.VMEM((shards,) + stats.shape, F32), dma((shards,)), dma((shards,)),
+        ],
+        compiler_params=pltpu.CompilerParams(collective_id=1, has_side_effects=True),
+        name="total_exchange",
+    )(stats)
+
+
+def local_fast(
+    queries, new_keys, new_values, cache_keys, cache_values, lengths, parents, tree_tokens,
+    residual, out_weight, norm_gain, vocab_weight,
+):
+    reqs, tree, width = queries.shape
+    tokens = reqs * tree
+    shard = lax.axis_index("mp")
+    shards = lax.axis_size("mp")
+    groups = lax.axis_size("dp")
+    ncol = width // shards
+    anc = ancestor_mask(parents).astype(F32)
+    part = attention(
+        shards, queries, new_keys, new_values, cache_keys, cache_values, lengths, anc
+    ).reshape(shards, tokens // shards, width + 128)
+    res = lax.dynamic_slice_in_dim(residual.reshape(tokens, width), shard * ncol, ncol, 1)
+    hidden = hidden_of(shards, groups, part, out_weight, res)
+
+    vocab = vocab_weight.shape[1]
+    column = tree_tokens - shard * vocab
+    column = jnp.where((column >= 0) & (column < vocab), column, -1)
+    idx = jnp.arange(tree, dtype=jnp.int32)[None, :]
+    by_one = (parents == idx - 1) & (idx > 0)
+    by_two = (parents == idx - 2) & (idx > 1)
+
+    def ahead(x, n):
+        return jnp.pad(x[:, n:], ((0, 0), (0, n)), constant_values=-1)
+
+    first = jnp.where(idx == 0, column, -1)
+    marks = jnp.stack(
+        [ahead(jnp.where(by_one, column, -1), 1), ahead(jnp.where(by_two, column, -1), 2), first], -1
+    ).reshape(tokens, 3)
+    marks = jnp.pad(marks, ((0, 0), (0, 125)), constant_values=-1)
+    stats = score(hidden, norm_gain.reshape(1, width), marks, vocab_weight)
+    total = total_of(shards, stats).reshape(8, reqs, tree)
+
+    def behind(x, n):
+        return jnp.pad(x[:, : tree - n], ((0, 0), (n, 0)))
+
+    sums = total[0]
+    picked = jnp.where(idx == 0, total[3], jnp.where(by_one, behind(total[1], 1), behind(total[2], 2)))
+    norm = jnp.where(idx == 0, sums, jnp.where(by_one, behind(sums, 1), behind(sums, 2)))
+    return (hidden.reshape(reqs, tree, width), picked - jnp.log(norm))
+
+
+def local_plain(
     queries,
     new_keys,
     new_values,
@@ -98,6 +544,21 @@
     return (hidden.reshape(reqs, tree, width), node_logprob)
 
 
+def local(*args):
+    queries, vocab_weight = args[0], args[-1]
+    reqs, tree, width = queries.shape
+    shards = lax.axis_size("mp")
+    fits = (
+        (reqs * tree) % (shards * 16) == 0
+        and width % (shards * 128) == 0
+        and width == HEADS * 128
+        and tree % 16 == 0
+        and shards % 2 == 0
+        and shards >= 8
+    )
+    return (local_fast if fits else local_plain)(*args)
+
+
 def solution(mesh):
     placed = (
         P("dp", None, None),

time: 188 us -> 116 us (0.62)
  Pallas kernels: 0 us -> 106 us
  waiting for transfers between devices: 75.8 us -> 0 us
  blocking collectives: 47.5 us -> 0 us
  matrix products: 35.8 us -> 2.71 us
  between operations: 15.7 us -> 0.87 us
  local copies, waits for them, and re-layouts: 10.7 us -> 5.01 us
    pallas_call x0 -> x4, Pallas kernels: none -> 106 us  [the longest x1 66.2 us: hidden_of(): pl.pallas_call(functools.partial(hidden_kernel, chips, groups), in_specs=...]
    psum x1 -> x0, waiting for transfers between devices: 75.3 us -> none  [local(): lax.psum((cache_num.reshape(tokens, width), cache_den), 'mp')]
    psum x2 -> x0, blocking collectives: 47.5 us -> none  [the longest x1 32.3 us: local(): lax.psum((cache_num.reshape(tokens, width), cache_den), 'mp')]
    dot_general x6 -> x0, matrix products: 34 us -> none  [the longest x1 10.5 us: local(): logits = jnp.dot(normed, vocab_weight, preferred_element_type=jnp.float32)]
    gather x2 -> x0, local copies, waits for them, and re-layouts: 9.16 us -> none  [the longest x1 6.37 us: local(): logits[parent_rows, jnp.clip(column, 0, vocab_dev - 1)]]
    unnamed x14 -> x21, local copies, waits for them, and re-layouts: 0.09 us -> 3.23 us
  transfers between devices with their start and end apart: 2 -> 0, of which waited for: 1 -> 0; matrix products, arithmetic and copies ran while one was open for 6% -> 0% of each run, Pallas kernels for 0% -> 0%
where the time goes in v1:
time: 116 us; the launch traced here: 115 us
  Pallas kernels  106 us (91%)
  local copies, waits for them, and re-layouts  5.01 us (4%)
  matrix products  2.71 us (2%)
    pallas_call x1, Pallas kernels, hidden_of(): pl.pallas_call(functools.partial(hidden_kernel, chips, groups), in_specs=...  66.2 us
    pallas_call x1, Pallas kernels, attention(): pl.pallas_call(functools.partial(attention_kernel, shards), grid=(reqs,),...  23.3 us
    pallas_call x1, Pallas kernels, score(): pl.pallas_call(functools.partial(score_kernel, vocab), grid=(pl.cdiv(voca...  9.27 us
    pallas_call x1, Pallas kernels, total_of(): pl.pallas_call(functools.partial(total_kernel, shards), in_specs=[vmem],...  7.25 us
    unnamed x21, local copies, waits for them, and re-layouts  3.23 us
    dot_general x6, matrix products, ancestor_mask(): jnp.einsum('rij,rjk->rik', links, links, precision=lax.Precision.HIGHEST)  2.71 us

profile of v1, /device:TPU:0, one launch (start us, length us, event | category | flops | bytes accessed | tf_op | source)
XLA Modules:
  0.0 115.3 jit_solution(1199474599558042588)
XLA Ops:
  0.6 0.0 copy-start
  0.7 0.0 copy-start.2
  0.7 0.0 copy-start.3
  0.7 0.0 copy-start.7
  0.7 1.1 convolution_minimum_fusion.5
  1.8 0.3 convolution_minimum_fusion.4
  2.2 0.3 convolution_minimum_fusion.3
  2.5 0.3 convolution_minimum_fusion.2
  2.8 0.3 convolution_minimum_fusion.1
  3.1 0.3 fusion.1.anc_ref
  3.4 0.0 copy-done.2
  3.5 0.0 copy-done.3
  3.5 0.0 copy-done.7
  3.5 0.0 copy-start.4
  3.5 23.3 %attention_part.1.part = bf16[8,48,2176]{2,1,0:T(8,128)(2,1)} custom-call(s32[8]{0:T(128)S(1)} %copy-done.7, bf16[8,48,2048]{2,1,0:T(8,128)(2,1)S(1)} %copy-done.2, bf16[8,128,2048]{2,1,0:T(8,128)(2,1)} %k_ref.1, bf16[8,128,2048]{2,1,0:T(8,128)(2,1)} %v_ref.1, bf16[8,48,2048]{2,1,0:T(8,128)(2,1)S(1)} %copy-done.3, bf16[8,48,2048]{2,1,0:T(8,128)(2,1)} %nv_ref.1, ...), custom_call_target="tpu_custom_call" | custom-call | tf_op jit(solution)/shard_map/attention_part/pallas_call | solution.py:83
  26.8 0.0 copy-done
  26.8 0.0 copy-done.4
  26.8 0.0 copy-start.1
  26.8 1.4 %copy-done.1 = bf16[8,48,2176]{2,1,0:T(8,128)(2,1)S(1)} copy-done((bf16[8,48,2176]{2,1,0:T(8,128)(2,1)S(1)}, bf16[8,48,2176]{2,1,0:T(8,128)(2,1)}, u32[]{:S(2)}) %copy-start.1) | copy-done | bytes 1671192
  28.3 0.0 copy-start.8
  28.3 0.0 copy-start.9
  28.3 0.0 copy-start.6
  28.3 66.2 %hidden_exchange.1.h_ref = bf16[384,2048]{1,0:T(8,128)(2,1)S(1)} custom-call(bf16[8,48,2176]{2,1,0:T(8,128)(2,1)S(1)} %copy-done.1, bf16[64,2048]{1,0:T(8,128)(2,1)S(1)} %copy-done.4, bf16[384,256]{1,0:T(8,128)(2,1)S(1)} %constant_dynamic-slice_fusion.res_ref), custom_call_target="tpu_custom_call" | custom-call | tf_op jit(solution)/shard_map/hidden_exchange/pallas_call | solution.py:302
  94.5 0.0 copy-done.8
  94.5 0.0 copy-done.9
  94.5 0.1 stack.14
  94.6 0.1 slice.35
  94.7 0.1 stack.13
  94.8 0.1 slice.34
  94.8 0.1 stack.12
  94.9 0.1 copy.17
  95.1 0.0 copy-done.6
  95.1 9.3 %score_part.1.x_ref = f32[8,384]{1,0:T(8,128)S(1)} custom-call(bf16[384,2048]{1,0:T(8,128)(2,1)S(1)} %hidden_exchange.1.h_ref, f32[1,2048]{1,0:T(1,128)S(1)} %bitcast.19, s32[384,128]{1,0:T(8,128)S(1)} %pad.28.t_ref, bf16[2048,2432]{1,0:T(8,128)(2,1)} %w_ref.3), custom_call_target="tpu_custom_call" | custom-call | tf_op jit(solution)/shard_map/score_part/pallas_call | solution.py:366
  104.4 0.0 copy-start.5
  104.4 0.6 copy-done.5
  105.0 7.3 %total_exchange.1 = f32[8,384]{1,0:T(8,128)} custom-call(f32[8,384]{1,0:T(8,128)} %copy-done.5), custom_call_target="tpu_custom_call" | custom-call | tf_op jit(solution)/shard_map/total_exchange/pallas_call | solution.py:412
  112.3 0.9 slice_reduce_fusion.2
  113.2 0.1 squeeze.15
  113.2 0.1 squeeze.12
  113.3 0.1 squeeze.14
  113.4 0.1 squeeze.13
  113.5 0.7 log_subtract_fusion
  114.2 1.1 copy.19
  (10 shorter events, 0.1 us)
Async XLA Ops:
  0.6 26.2 %copy-start = (bf16[8,48,2048]{2,1,0:T(8,128)(2,1)S(1)}, bf16[8,48,2048]{2,1,0:T(8,128)(2,1)}, u32[]{:S(2)}) copy-start(bf16[8,48,2048]{2,1,0:T(8,128)(2,1)} %param.20) | copy-start | bytes 4718596
  0.7 2.8 %copy-start.2 = (bf16[8,48,2048]{2,1,0:T(8,128)(2,1)S(1)}, bf16[8,48,2048]{2,1,0:T(8,128)(2,1)}, u32[]{:S(2)}) copy-start(bf16[8,48,2048]{2,1,0:T(8,128)(2,1)} %q_ref.1) | copy-start | bytes 4718596
  0.7 2.8 %copy-start.3 = (bf16[8,48,2048]{2,1,0:T(8,128)(2,1)S(1)}, bf16[8,48,2048]{2,1,0:T(8,128)(2,1)}, u32[]{:S(2)}) copy-start(bf16[8,48,2048]{2,1,0:T(8,128)(2,1)} %nk_ref.1) | copy-start | bytes 4718596
  0.7 2.8 %copy-start.7 = (s32[8]{0:T(128)S(1)}, s32[8]{0:T(128)}, u32[]{:S(2)}) copy-start(s32[8]{0:T(128)} %len_ref.1) | copy-start | bytes 100
  3.5 23.3 %copy-start.4 = (bf16[64,2048]{1,0:T(8,128)(2,1)S(1)}, bf16[64,2048]{1,0:T(8,128)(2,1)}, u32[]{:S(2)}) copy-start(bf16[64,2048]{1,0:T(8,128)(2,1)} %w_ref.2) | copy-start | bytes 786436
  26.8 1.4 %copy-start.1 = (bf16[8,48,2176]{2,1,0:T(8,128)(2,1)S(1)}, bf16[8,48,2176]{2,1,0:T(8,128)(2,1)}, u32[]{:S(2)}) copy-start(bf16[8,48,2176]{2,1,0:T(8,128)(2,1)} %attention_part.1.part) | copy-start | bytes 5013508
  28.3 66.2 %copy-start.8 = (s32[8,48]{1,0:T(8,128)S(1)}, s32[8,48]{1,0:T(8,128)}, u32[]{:S(2)}) copy-start(s32[8,48]{1,0:T(8,128)} %param.18) | copy-start | bytes 4612
  28.3 66.2 %copy-start.9 = (s32[8,48]{1,0:T(8,128)S(1)}, s32[8,48]{1,0:T(8,128)}, u32[]{:S(2)}) copy-start(s32[8,48]{1,0:T(8,128)} %param.19) | copy-start | bytes 4612
  28.3 66.8 %copy-start.6 = (f32[2048]{0:T(1024)S(1)}, f32[2048]{0:T(1024)}, u32[]{:S(2)}) copy-start(f32[2048]{0:T(1024)} %param.22) | copy-start | bytes 24580
  104.4 0.6 copy-start.5

commit v2 on v1

v2 whole, which is shorter than its diff:
```python
import functools

import jax
import jax.numpy as jnp
from jax import lax
from jax.experimental import pallas as pl
from jax.experimental.pallas import tpu as pltpu
from jax.sharding import PartitionSpec as P

HEADS = 16
SINK = 4
F32 = jnp.float32
BF16 = jnp.bfloat16
MESH = pl.DeviceIdType.MESH
VMEM_LIMIT = 50 * 1024 * 1024


def ancestor_mask(parents):
    tree = parents.shape[-1]
    idx = jnp.arange(tree, dtype=jnp.int32)
    links = (
        (idx[None, :, None] == idx[None, None, :]) | (parents[:, :, None] == idx[None, None, :])
    ).astype(F32)
    for _ in range((tree - 1).bit_length()):
        links = jnp.minimum(
            jnp.einsum("rij,rjk->rik", links, links, precision=lax.Precision.HIGHEST), 1.0
        )
    return links > 0.5


def attention_kernel(
    shards, len_ref, q_ref, k_ref, v_ref, nk_ref, nv_ref, par_ref, o_ref, chain
):
    req = pl.program_id(0)
    shard = lax.axis_index("mp")
    slots = k_ref.shape[1]
    tree, width = q_ref.shape[1:]
    reqs = par_ref.shape[0]
    hd = width // HEADS
    scale = hd ** (-0.5)
    cap = slots * shards
    length = len_ref[req]
    start = shard * slots
    tree_shard = max(shards // 8, 1)
    seen = (start < length) & ((start < SINK) | (start + slots > length - cap // 2))

    def attend(keys, values, mask):
        lane = lax.broadcasted_iota(jnp.int32, (tree, 128), 1)
        low = lax.broadcasted_iota(jnp.int32, (tree, 2 * hd), 1) < hd
        mask2 = jnp.concatenate([mask, mask], 0)
        den = jnp.zeros((tree, 128), F32)
        pairs = HEADS // 2
        for group in range(0, pairs, 4):
            scores = []
            for p in range(group, group + 4):
                cols = slice(2 * p * hd, 2 * (p + 1) * hd)
                q = q_ref[0, :, cols]
                both = jnp.concatenate(
                    [jnp.where(low, q, jnp.zeros_like(q)), jnp.where(low, jnp.zeros_like(q), q)], 0
                )
                scores.append(
                    lax.dot_general(
                        both, keys[0, :, cols], (((1,), (1,)), ((), ())),
                        preferred_element_type=F32,
                    )
                )
            es = [jnp.where(mask2 > 0.5, jnp.exp(s * scale), 0.0) for s in scores]
            for n, e in enumerate(es):
                p = group + n
                cols = slice(2 * p * hd, 2 * (p + 1) * hd)
                num = jnp.dot(e.astype(BF16), values[0, :, cols], preferred_element_type=F32)
                o_ref[0, :, 2 * p * hd : (2 * p + 1) * hd] = num[:tree, :hd].astype(BF16)
                o_ref[0, :, (2 * p + 1) * hd : 2 * (p + 1) * hd] = num[tree:, hd:].astype(BF16)
                d = jnp.sum(e, -1, keepdims=True)
                den = jnp.where(lane == 2 * p, d[:tree], den)
                den = jnp.where(lane == 2 * p + 1, d[tree:], den)
        o_ref[0, :, width:] = den.astype(BF16)

    @pl.when((shard == tree_shard) & (req == 0))
    def _():
        node = lax.broadcasted_iota(jnp.int32, (reqs, 128), 1)
        rows = []
        for j in range(tree):
            row = jnp.where(node == j, 1.0, 0.0)
            if j == 1:
                row = row + rows[0]
            elif j > 1:
                row = row + jnp.where(par_ref[:, j : j + 1] == j - 1, rows[j - 1], rows[j - 2])
            rows.append(row)
            chain[j] = row

    @pl.when(shard == tree_shard)
    def _():
        attend(nk_ref, nv_ref, chain[:, req, :][:, :tree])

    @pl.when((shard != tree_shard) & seen)
    def _():
        pos = start + lax.broadcasted_iota(jnp.int32, (tree, slots), 1)
        mask = (pos < length) & ((pos < SINK) | (pos >= length - cap // 2))
        attend(k_ref, v_ref, jnp.where(mask, 1.0, 0.0))

    @pl.when((shard != tree_shard) & jnp.logical_not(seen))
    def _():
        o_ref[...] = jnp.zeros_like(o_ref)


def attention(shards, queries, new_keys, new_values, cache_keys, cache_values, lengths, parents):
    reqs, tree, width = queries.shape
    slots = cache_keys.shape[1]

    def block(rows, cols):
        return pl.BlockSpec((1, rows, cols), lambda r: (r, 0, 0))

    return pl.pallas_call(
        functools.partial(attention_kernel, shards),
        grid=(reqs,),
        in_specs=[
            pl.BlockSpec(memory_space=pltpu.SMEM),
            block(tree, width),
            block(slots, width),
            block(slots, width),
            block(tree, width),
            block(tree, width),
            pl.BlockSpec((reqs, tree), lambda r: (0, 0)),
        ],
        out_specs=block(tree, width + 128),
        out_shape=jax.ShapeDtypeStruct((reqs, tree, width + 128), BF16),
        scratch_shapes=[pltpu.VMEM((tree, reqs, 128), F32)],
        compiler_params=pltpu.CompilerParams(vmem_limit_bytes=VMEM_LIMIT),
        name="attention_part",
    )(lengths, queries, cache_keys, cache_values, new_keys, new_values, parents)


def when(cond, fn):
    pl.when(cond)(fn)


class Line:
    def __init__(self, chips, at, recv, send_r, send_l, send_s):
        me = lax.axis_index("mp")
        self.chips, self.at, self.recv = chips, at, recv
        self.sends = send_r, send_l, send_s
        self.me, self.c, self.z = me, lax.rem(me, 2), lax.div(me, 2)
        self.sib = 2 * self.z + 1 - self.c

    def copy(self, slot, sem, to):
        return pltpu.make_async_remote_copy(
            src_ref=self.at(slot), dst_ref=self.at(slot), send_sem=sem,
            recv_sem=self.recv.at[slot], device_id={"mp": to}, device_id_type=MESH,
        )

    def right(self, k):
        return self.copy(2 * (self.z - k) + self.c, self.sends[0].at[k], self.me + 2)

    def left(self, k):
        return self.copy(2 * (self.z + k) + self.c, self.sends[1].at[k], self.me - 2)

    def pair(self, zs):
        return self.copy(2 * zs + self.c, self.sends[2].at[zs], self.sib)

    def start(self):
        when(self.z < self.chips - 1, lambda: self.right(0).start())
        when(self.z > 0, lambda: self.left(0).start())
        self.pair(self.z).start()

    def forward(self):
        z, chips = self.z, self.chips
        for k in range(1, chips):

            @pl.when(z - k >= 0)
            def _():
                self.right(k).wait_recv()
                when(z < chips - 1, lambda: self.right(k).start())
                self.pair(z - k).start()

            @pl.when(z + k <= chips - 1)
            def _():
                self.left(k).wait_recv()
                when(z > 0, lambda: self.left(k).start())
                self.pair(z + k).start()

        for zs in range(chips):
            self.copy(2 * zs + 1 - self.c, self.sends[2].at[zs], self.sib).wait_recv()

    def finish(self):
        z, chips = self.z, self.chips
        for k in range(chips):
            when((z - k >= 0) & (z < chips - 1), lambda: self.right(k).wait_send())
            when((z + k <= chips - 1) & (z > 0), lambda: self.left(k).wait_send())
        for zs in range(chips):
            self.pair(zs).wait_send()


CHUNK = 16


def hidden_kernel(
    chips, groups, part, w_ref, res_ref, out_ref,
    own_buf, sib_buf, from_l, from_r, acc, tot, att, wcol, hcol,
    own_s, sib_s, sib_r, fl_r, fr_r, acc_s, g1_r, g1_a, g1_b, g1_c, g2_r, g2_a, g2_b, g2_c,
    w1_s, w1_r, w2_s, w2_r, wown_s,
):
    shards = 2 * chips
    me = lax.axis_index("mp")
    grp = lax.axis_index("dp")
    c, z = lax.rem(me, 2), lax.div(me, 2)
    sib = 2 * z + 1 - c
    width = att.shape[-1]
    hd = width // HEADS
    ncol = wcol.shape[-1]
    chunks = att.shape[1] // CHUNK

    def rows(i):
        return pl.ds(i * CHUNK, CHUNK)

    def columns(j):
        return pl.ds(pl.multiple_of(j * ncol, 128), ncol)

    barrier = pltpu.get_barrier_semaphore()
    for k in range(1, shards):
        pl.semaphore_signal(
            barrier, inc=1, device_id={"mp": lax.rem(me + k, shards)}, device_id_type=MESH
        )
    for k in range(1, groups):
        pl.semaphore_signal(
            barrier, inc=1, device_id={"dp": lax.rem(grp + k, groups)}, device_id_type=MESH
        )

    order = []
    for k in range(chips):
        for zd in (chips - 1 - k, k):
            if zd not in order:
                order.append(zd)

    def mine(i, zd):
        return pltpu.make_async_copy(
            part.at[2 * zd + c, rows(i)], own_buf.at[zd, rows(i)], own_s.at[i, zd]
        )

    for i in range(chunks):
        for zd in order:
            mine(i, zd).start()
    own_w = pltpu.make_async_copy(w_ref.at[:, columns(me)], wcol.at[grp, me], wown_s)
    own_w.start()

    pl.semaphore_wait(barrier, shards - 1 + groups - 1)

    def pair(i, zd):
        return pltpu.make_async_remote_copy(
            src_ref=part.at[2 * zd + 1 - c, rows(i)], dst_ref=sib_buf.at[zd, rows(i)],
            send_sem=sib_s.at[i, zd], recv_sem=sib_r.at[i, zd],
            device_id={"mp": sib}, device_id_type=MESH,
        )

    for i in range(chunks):
        for zd in order:
            pair(i, zd).start()

    def w_mp(k):
        to = lax.rem(me + k, shards)
        return pltpu.make_async_remote_copy(
            src_ref=w_ref.at[:, columns(to)], dst_ref=wcol.at[grp, me], send_sem=w1_s.at[k],
            recv_sem=w1_r.at[k], device_id={"mp": to}, device_id_type=MESH,
        )

    def w_dp(k, src):
        return pltpu.make_async_remote_copy(
            src_ref=wcol.at[src], dst_ref=wcol.at[src], send_sem=w2_s.at[k],
            recv_sem=w2_r.at[k], device_id={"dp": lax.rem(grp + k, groups)}, device_id_type=MESH,
        )

    def pass_on(i, zd, buf, sems, to):
        return pltpu.make_async_remote_copy(
            src_ref=acc.at[zd, rows(i)], dst_ref=buf.at[zd, rows(i)], send_sem=acc_s.at[i, zd],
            recv_sem=sems.at[i, zd], device_id={"mp": to}, device_id_type=MESH,
        )

    def both(i, zd):
        return own_buf[zd, rows(i)].astype(F32) + sib_buf[zd, rows(i)].astype(F32)

    def arrive(i, zd):
        mine(i, zd).wait()
        pair(i, zd).wait_recv()

    def step(i, zd, buf, sems, first, to):
        arrive(i, zd)

        @pl.when(first)
        def _():
            acc[zd, rows(i)] = both(i, zd).astype(BF16)

        @pl.when(jnp.logical_not(first))
        def _():
            pass_on(i, zd, buf, sems, to).wait_recv()
            acc[zd, rows(i)] = (both(i, zd) + buf[zd, rows(i)].astype(F32)).astype(BF16)

        pass_on(i, zd, buf, sems, to).start()

    def sums(i):
        for k in range(chips - 1):
            rd, ld = chips - 1 - k, k
            when(rd > z, functools.partial(step, i, rd, from_l, fl_r, z == 0, me + 2))
            when(ld < z, functools.partial(step, i, ld, from_r, fr_r, z == chips - 1, me - 2))

    first = [
        Line(chips, lambda j, i=i: att.at[j, rows(i)], g1_r.at[i], g1_a.at[i], g1_b.at[i], g1_c.at[i])
        for i in range(chunks)
    ]
    second = [
        Line(chips, lambda j, i=i: hcol.at[j, i], g2_r.at[i], g2_a.at[i], g2_b.at[i], g2_c.at[i])
        for i in range(chunks)
    ]

    def attended(i):
        arrive(i, z)
        tot[...] = both(i, z)

        @pl.when(z > 0)
        def _():
            pass_on(i, z, from_l, fl_r, me).wait_recv()
            tot[...] += from_l[z, rows(i)].astype(F32)

        @pl.when(z < chips - 1)
        def _():
            pass_on(i, z, from_r, fr_r, me).wait_recv()
            tot[...] += from_r[z, rows(i)].astype(F32)

        for h in range(HEADS):
            cols = slice(h * hd, (h + 1) * hd)
            att[me, rows(i), cols] = (tot[:, cols] / tot[:, width + h : width + h + 1]).astype(BF16)
        first[i].start()

    def project(i):
        first[i].forward()
        if i == 0:
            for k in range(1, groups):
                w_dp(k, lax.rem(grp + groups - k, groups)).wait_recv()
        projected = jnp.dot(
            att[:, rows(i), :].reshape(shards * CHUNK, width),
            wcol[...].reshape(width, ncol),
            preferred_element_type=F32,
        )
        res = res_ref[:, rows(i), :].reshape(shards * CHUNK, ncol)
        hcol[me, i] = (res.astype(F32) + projected).astype(BF16)
        second[i].start()

    def place(i):
        second[i].forward()
        for j in range(shards):
            for t in range(shards):
                out_ref[t, rows(i), j * ncol : (j + 1) * ncol] = hcol[
                    j, i, t * CHUNK : (t + 1) * CHUNK
                ]

    sums(0)
    for k in range(1, shards):
        w_mp(k).start()
    for i in range(chunks):
        if i + 1 < chunks:
            sums(i + 1)
        attended(i)
        if i == 0:
            for k in range(1, shards):
                w_mp(k).wait_recv()
            own_w.wait()
            for k in range(1, groups):
                w_dp(k, grp).start()
        if i >= 1:
            project(i - 1)
        if i >= 2:
            place(i - 2)
    project(chunks - 1)
    if chunks >= 2:
        place(chunks - 2)
    place(chunks - 1)

    for i in range(chunks):
        first[i].finish()
        second[i].finish()
        for zd in range(chips):
            pair(i, zd).wait_send()
            when(zd != z, lambda: pass_on(i, zd, from_l, fl_r, me).wait_send())
    for k in range(1, shards):
        w_mp(k).wait_send()
    for k in range(1, groups):
        w_dp(k, grp).wait_send()


def hidden_of(shards, groups, part, out_weight, res):
    own, width = part.shape[1], out_weight.shape[1]
    wide = part.shape[2]
    ncol = width // shards
    chips = shards // 2
    chunks = own // CHUNK
    dma = pltpu.SemaphoreType.DMA
    gather_sems = [dma((chunks, shards))] + [dma((chunks, chips))] * 3
    vmem = pl.BlockSpec(memory_space=pltpu.VMEM)
    return pl.pallas_call(
        functools.partial(hidden_kernel, chips, groups),
        in_specs=[pl.BlockSpec(memory_space=pl.ANY), vmem, vmem],
        out_specs=vmem,
        out_shape=jax.ShapeDtypeStruct((shards, own, width), BF16),
        scratch_shapes=[
            pltpu.VMEM((chips, own, wide), BF16),
            pltpu.VMEM((chips, own, wide), BF16),
            pltpu.VMEM((chips, own, wide), BF16),
            pltpu.VMEM((chips, own, wide), BF16),
            pltpu.VMEM((chips, own, wide), BF16),
            pltpu.VMEM((CHUNK, wide), F32),
            pltpu.VMEM((shards, own, width), BF16),
            pltpu.VMEM((groups, shards, out_weight.shape[0], ncol), BF16),
            pltpu.VMEM((shards, chunks, shards * CHUNK, ncol), BF16),
            *[dma((chunks, chips))] * 6,
            *gather_sems,
            *gather_sems,
            dma((shards,)), dma((shards,)), dma((groups,)), dma((groups,)), dma,
        ],
        compiler_params=pltpu.CompilerParams(
            collective_id=0, has_side_effects=True, vmem_limit_bytes=VMEM_LIMIT
        ),
        name="hidden_exchange",
    )(part, out_weight, res)


def score_kernel(vocab, shards, h_ref, g_ref, t_ref, w_ref, o_ref, normed, sums, stats, slots, send, recv):
    step = pl.program_id(0)
    tile = w_ref.shape[1]
    rows = h_ref.shape[0]
    me = lax.axis_index("mp")
    barrier = pltpu.get_barrier_semaphore()

    @pl.when(step == 0)
    def _():
        for k in range(1, shards):
            pl.semaphore_signal(
                barrier, inc=1, device_id={"mp": lax.rem(me + k, shards)}, device_id_type=MESH
            )
        h = h_ref[...].astype(F32)
        normed[...] = (
            h * lax.rsqrt(jnp.mean(h * h, -1, keepdims=True) + 1e-06) * g_ref[...]
        ).astype(BF16)
        sums[...] = jnp.zeros_like(sums)

    logits = jnp.dot(normed[...], w_ref[...], preferred_element_type=F32)
    lane = lax.broadcasted_iota(jnp.int32, (rows, 128), 1)
    marks = [t_ref[:, n : n + 1] for n in range(3)]
    new = [jnp.zeros((rows, 128), F32) for _ in range(4)]
    for b in range(tile // 128):
        col = step * tile + b * 128 + lane
        x = logits[:, b * 128 : (b + 1) * 128]
        new[0] += jnp.where(col < vocab, jnp.exp(x), 0.0)
        for n in range(3):
            new[n + 1] += jnp.where(col == marks[n], x, 0.0)
    for n in range(4):
        sums[n] += new[n]

    @pl.when(step == pl.num_programs(0) - 1)
    def _():
        stat = jnp.zeros((rows, 128), F32)
        for n in range(4):
            stat = jnp.where(lane == n, jnp.sum(sums[n], -1, keepdims=True), stat)
        stats[...] = jnp.transpose(stat)[:8]
        pl.semaphore_wait(barrier, shards - 1)

        def copy(k):
            return pltpu.make_async_remote_copy(
                src_ref=stats, dst_ref=slots.at[k], send_sem=send.at[k], recv_sem=recv.at[k],
                device_id={"mp": lax.rem(me + k, shards)}, device_id_type=MESH,
            )

        for k in range(1, shards):
            copy(k).start()
        total = stats[...]
        for k in range(1, shards):
            copy(k).wait_recv()
            total = total + slots[k]
        o_ref[...] = total
        for k in range(1, shards):
            copy(k).wait_send()


def score(shards, hidden, gain, marks, vocab_weight):
    rows, width = hidden.shape
    vocab = vocab_weight.shape[1]
    tile = 512
    dma = pltpu.SemaphoreType.DMA
    return pl.pallas_call(
        functools.partial(score_kernel, vocab, shards),
        grid=(pl.cdiv(vocab, tile),),
        in_specs=[
            pl.BlockSpec((rows, width), lambda i: (0, 0)),
            pl.BlockSpec((1, width), lambda i: (0, 0)),
            pl.BlockSpec((rows, 128), lambda i: (0, 0)),
            pl.BlockSpec((width, tile), lambda i: (0, i)),
        ],
        out_specs=pl.BlockSpec((8, rows), lambda i: (0, 0)),
        out_shape=jax.ShapeDtypeStruct((8, rows), F32),
        scratch_shapes=[
            pltpu.VMEM((rows, width), BF16),
            pltpu.VMEM((4, rows, 128), F32),
            pltpu.VMEM((8, rows), F32),
            pltpu.VMEM((shards, 8, rows), F32),
            dma((shards,)),
            dma((shards,)),
        ],
        compiler_params=pltpu.CompilerParams(
            collective_id=1, has_side_effects=True, vmem_limit_bytes=VMEM_LIMIT
        ),
        name="score_exchange",
    )(hidden, gain, marks, vocab_weight)


def local_fast(
    queries, new_keys, new_values, cache_keys, cache_values, lengths, parents, tree_tokens,
    residual, out_weight, norm_gain, vocab_weight,
):
    reqs, tree, width = queries.shape
    tokens = reqs * tree
    shard = lax.axis_index("mp")
    shards = lax.axis_size("mp")
    groups = lax.axis_size("dp")
    ncol = width // shards
    part = attention(
        shards, queries, new_keys, new_values, cache_keys, cache_values, lengths, parents
    ).reshape(shards, tokens // shards, width + 128)
    res = lax.dynamic_slice_in_dim(residual.reshape(tokens, width), shard * ncol, ncol, 1)
    res = res.reshape(shards, tokens // shards, ncol)
    hidden = hidden_of(shards, groups, part, out_weight, res).reshape(tokens, width)

    vocab = vocab_weight.shape[1]
    column = tree_tokens - shard * vocab
    column = jnp.where((column >= 0) & (column < vocab), column, -1)
    idx = jnp.arange(tree, dtype=jnp.int32)[None, :]
    by_one = (parents == idx - 1) & (idx > 0)
    by_two = (parents == idx - 2) & (idx > 1)

    def ahead(x, n):
        return jnp.pad(x[:, n:], ((0, 0), (0, n)), constant_values=-1)

    first = jnp.where(idx == 0, column, -1)
    marks = jnp.stack(
        [ahead(jnp.where(by_one, column, -1), 1), ahead(jnp.where(by_two, column, -1), 2), first], -1
    ).reshape(tokens, 3)
    marks = jnp.pad(marks, ((0, 0), (0, 125)), constant_values=-1)
    stats = score(shards, hidden, norm_gain.reshape(1, width), marks, vocab_weight)
    total = stats.reshape(8, reqs, tree)

    def behind(x, n):
        return jnp.pad(x[:, : tree - n], ((0, 0), (n, 0)))

    sums = total[0]
    picked = jnp.where(idx == 0, total[3], jnp.where(by_one, behind(total[1], 1), behind(total[2], 2)))
    norm = jnp.where(idx == 0, sums, jnp.where(by_one, behind(sums, 1), behind(sums, 2)))
    return (hidden.reshape(reqs, tree, width), picked - jnp.log(norm))


def local_plain(
    queries,
    new_keys,
    new_values,
    cache_keys,
    cache_values,
    lengths,
    parents,
    tree_tokens,
    residual,
    out_weight,
    norm_gain,
    vocab_weight,
):
    reqs, tree, width = queries.shape
    slots = cache_keys.shape[1]
    head_dim = width // HEADS
    scale = head_dim ** (-0.5)
    shard = lax.axis_index("mp")
    shards = lax.axis_size("mp")
    tokens = reqs * tree
    window = slots * shards // 2
    positions = shard * slots + jnp.arange(slots, dtype=jnp.int32)
    visible = (positions[None, :] < lengths[:, None]) & (
        (positions[None, :] < SINK) | (positions[None, :] >= lengths[:, None] - window)
    )
    q4 = queries.reshape(reqs, tree, HEADS, head_dim)
    k4 = cache_keys.reshape(reqs, slots, HEADS, head_dim)
    v4 = cache_values.reshape(reqs, slots, HEADS, head_dim)
    cache_e = jnp.where(
        visible[:, None, None, :],
        jnp.exp(jnp.einsum("rihd,rshd->rhis", q4, k4, preferred_element_type=jnp.float32) * scale),
        0.0,
    )
    cache_den = jnp.sum(cache_e, -1)
    cache_num = jnp.einsum(
        "rhis,rshd->rihd", cache_e.astype(jnp.bfloat16), v4, preferred_element_type=jnp.float32
    )
    ancestors = ancestor_mask(parents)
    nk4 = new_keys.reshape(reqs, tree, HEADS, head_dim)
    nv4 = new_values.reshape(reqs, tree, HEADS, head_dim)
    tree_e = jnp.where(
        ancestors[:, None],
        jnp.exp(jnp.einsum("rihd,rjhd->rhij", q4, nk4, preferred_element_type=jnp.float32) * scale),
        0.0,
    )
    tree_den = jnp.sum(tree_e, -1)
    tree_num = jnp.einsum(
        "rhij,rjhd->rihd", tree_e.astype(jnp.bfloat16), nv4, preferred_element_type=jnp.float32
    )
    flat_res = residual.reshape(tokens, width)
    num_all, den_all = lax.psum((cache_num.reshape(tokens, width), cache_den), "mp")
    denom = jnp.transpose(den_all + tree_den, (0, 2, 1))
    numer = num_all.reshape(reqs, tree, HEADS, head_dim) + tree_num
    attended = (numer / denom[..., None]).astype(jnp.bfloat16).reshape(tokens, width)
    projected = jnp.dot(
        attended,
        lax.all_gather(out_weight, ("dp", "mp"), axis=0, tiled=True),
        preferred_element_type=jnp.float32,
    )
    hidden = (flat_res.astype(jnp.float32) + projected).astype(jnp.bfloat16)
    hfloat = hidden.astype(jnp.float32)
    normed = (
        hfloat * lax.rsqrt(jnp.mean(hfloat * hfloat, -1, keepdims=True) + 1e-06) * norm_gain
    ).astype(jnp.bfloat16)
    vocab_dev = vocab_weight.shape[1]
    logits = jnp.dot(normed, vocab_weight, preferred_element_type=jnp.float32)
    exp_sums = jnp.sum(jnp.exp(logits), -1)
    parent_rows = (jnp.arange(reqs, dtype=jnp.int32)[:, None] * tree + parents).reshape(-1)
    column = tree_tokens.reshape(-1) - shard * vocab_dev
    inside = (column >= 0) & (column < vocab_dev)
    picked = jnp.where(inside, logits[parent_rows, jnp.clip(column, 0, vocab_dev - 1)], 0.0)
    parent_sums = exp_sums[parent_rows]
    total_sums, total_picked = lax.psum((parent_sums, picked), "mp")
    node_logprob = (total_picked - jnp.log(total_sums)).reshape(reqs, tree)
    return (hidden.reshape(reqs, tree, width), node_logprob)


def local(*args):
    queries, vocab_weight = args[0], args[-1]
    reqs, tree, width = queries.shape
    shards = lax.axis_size("mp")
    fits = (
        (reqs * tree) % (shards * 16) == 0
        and width % (shards * 128) == 0
        and width == HEADS * 128
        and tree % 16 == 0
        and shards % 2 == 0
        and shards >= 8
    )
    return (local_fast if fits else local_plain)(*args)


def solution(mesh):
    placed = (
        P("dp", None, None),
        P("dp", None, None),
        P("dp", None, None),
        P("dp", "mp", None),
        P("dp", "mp", None),
        P("dp"),
        P("dp", None),
        P("dp", None),
        P("dp", None, None),
        P(("dp", "mp"), None),
        P(),
        P(None, "mp"),
    )
    return jax.shard_map(
        local,
        mesh=mesh,
        in_specs=placed,
        out_specs=(P("dp", None, None), P("dp", None)),
        check_vma=False,
    )
```

time: 116 us -> 108 us (0.931)
  Pallas kernels: 106 us -> 98.8 us
  local copies, waits for them, and re-layouts: 5.01 us -> 7.8 us
  matrix products: 2.71 us -> 0 us
    pallas_call x1, Pallas kernels: 23.3 us -> 9.29 us  [attention(): pl.pallas_call(functools.partial(attention_kernel, shards), grid=(reqs,),...]
    pallas_call x1, Pallas kernels: 66.2 us -> 76.1 us  [hidden_of(): pl.pallas_call(functools.partial(hidden_kernel, chips, groups), in_specs=...]
    unnamed x21, local copies, waits for them, and re-layouts: 3.23 us -> 6.87 us
    pallas_call x2 -> x1, Pallas kernels: 16.5 us -> 13.4 us  [score(): pl.pallas_call(functools.partial(score_kernel, vocab, shards), grid=(pl.c...]
    dot_general x6 -> x0, matrix products: 2.71 us -> none  [ancestor_mask(): jnp.einsum('rij,rjk->rik', links, links, precision=lax.Precision.HIGHEST)]
where the time goes in v2:
time: 108 us
  Pallas kernels  98.8 us (91%)
  local copies, waits for them, and re-layouts  7.8 us (7%)
    pallas_call x1, Pallas kernels, hidden_of(): pl.pallas_call(functools.partial(hidden_kernel, chips, groups), in_specs=...  76.1 us
    pallas_call x1, Pallas kernels, score(): pl.pallas_call(functools.partial(score_kernel, vocab, shards), grid=(pl.c...  13.4 us
    pallas_call x1, Pallas kernels, attention(): pl.pallas_call(functools.partial(attention_kernel, shards), grid=(reqs,),...  9.29 us
    unnamed x21, local copies, waits for them, and re-layouts  6.87 us

profile of v2, /device:TPU:0, one launch (start us, length us, event | category | flops | bytes accessed | tf_op | source)
XLA Modules:
  0.0 108.1 jit_solution(4921568581430164267)
XLA Ops:
  0.6 0.0 copy-start
  0.6 0.0 copy-start.2
  0.7 1.5 %copy-done.2 = bf16[8,48,2048]{2,1,0:T(8,128)(2,1)S(1)} copy-done((bf16[8,48,2048]{2,1,0:T(8,128)(2,1)S(1)}, bf16[8,48,2048]{2,1,0:T(8,128)(2,1)}, u32[]{:S(2)}) %copy-start.2) | copy-done | bytes 1572888
  2.2 0.0 copy-start.3
  2.2 1.4 %copy-done.3 = bf16[8,48,2048]{2,1,0:T(8,128)(2,1)S(1)} copy-done((bf16[8,48,2048]{2,1,0:T(8,128)(2,1)S(1)}, bf16[8,48,2048]{2,1,0:T(8,128)(2,1)}, u32[]{:S(2)}) %copy-start.3) | copy-done | bytes 1572888
  3.6 0.0 copy-start.5
  3.6 0.7 copy-done.5
  4.3 0.0 copy-start.8
  4.3 0.7 copy-done.8
  4.9 0.0 copy-start.4
  4.9 9.3 %attention_part.1.part = bf16[8,48,2176]{2,1,0:T(8,128)(2,1)} custom-call(s32[8]{0:T(128)S(1)} %copy-done.8, bf16[8,48,2048]{2,1,0:T(8,128)(2,1)S(1)} %copy-done.2, bf16[8,128,2048]{2,1,0:T(8,128)(2,1)} %k_ref.1, bf16[8,128,2048]{2,1,0:T(8,128)(2,1)} %v_ref.1, bf16[8,48,2048]{2,1,0:T(8,128)(2,1)S(1)} %copy-done.3, bf16[8,48,2048]{2,1,0:T(8,128)(2,1)} %nv_ref.1, ...), custom_call_target="tpu_custom_call" | custom-call | tf_op jit(solution)/shard_map/attention_part/pallas_call | solution.py:114
  14.2 0.0 copy-done
  14.2 0.0 copy-done.4
  14.3 0.0 copy-start.1
  14.3 1.4 %copy-done.1 = bf16[8,48,2176]{2,1,0:T(8,128)(2,1)S(1)} copy-done((bf16[8,48,2176]{2,1,0:T(8,128)(2,1)S(1)}, bf16[8,48,2176]{2,1,0:T(8,128)(2,1)}, u32[]{:S(2)}) %copy-start.1) | copy-done | bytes 1671192
  15.7 0.0 copy-start.6
  15.7 0.0 copy-start.9
  15.7 0.0 copy-start.7
  15.7 76.1 %hidden_exchange.1 = bf16[8,48,2048]{2,1,0:T(8,128)(2,1)S(1)} custom-call(bf16[8,48,2176]{2,1,0:T(8,128)(2,1)S(1)} %copy-done.1, bf16[64,2048]{1,0:T(8,128)(2,1)S(1)} %copy-done.4, bf16[8,48,256]{2,1,0:T(8,128)(2,1)S(1)} %bitcast.10), custom_call_target="tpu_custom_call" | custom-call | tf_op jit(solution)/shard_map/hidden_exchange/pallas_call | solution.py:398
  91.8 0.0 copy-done.6
  91.8 0.0 copy-done.9
  91.8 0.1 stack.14
  91.9 0.1 slice.35
  92.0 0.1 stack.13
  92.1 0.1 slice.34
  92.2 0.1 stack.12
  92.3 0.1 copy.17
  92.4 0.0 copy-done.7
  92.5 13.4 %score_exchange.1 = f32[8,384]{1,0:T(8,128)S(1)} custom-call(bf16[384,2048]{1,0:T(8,128)(2,1)S(1)} %bitcast.9, f32[1,2048]{1,0:T(1,128)S(1)} %bitcast.11, s32[384,128]{1,0:T(8,128)S(1)} %pad.28.t_ref, bf16[2048,2432]{1,0:T(8,128)(2,1)} %w_ref.3), custom_call_target="tpu_custom_call" | custom-call | tf_op jit(solution)/shard_map/score_exchange/pallas_call | solution.py:487
  105.9 0.1 squeeze.15
  106.0 0.1 squeeze.12
  106.1 0.1 squeeze.14
  106.1 0.1 squeeze.13
  106.2 0.7 log_subtract_fusion
  106.9 1.1 %copy.19 = bf16[8,48,2048]{2,1,0:T(8,128)(2,1)} copy(bf16[8,48,2048]{2,1,0:T(8,128)(2,1)S(1)} %hidden_exchange.1) | data formatting | bytes 3145728
  (10 shorter events, 0.1 us)
Async XLA Ops:
  0.6 13.6 %copy-start = (bf16[8,48,2048]{2,1,0:T(8,128)(2,1)S(1)}, bf16[8,48,2048]{2,1,0:T(8,128)(2,1)}, u32[]{:S(2)}) copy-start(bf16[8,48,2048]{2,1,0:T(8,128)(2,1)} %param.20) | copy-start | bytes 4718596
  0.6 1.5 %copy-start.2 = (bf16[8,48,2048]{2,1,0:T(8,128)(2,1)S(1)}, bf16[8,48,2048]{2,1,0:T(8,128)(2,1)}, u32[]{:S(2)}) copy-start(bf16[8,48,2048]{2,1,0:T(8,128)(2,1)} %q_ref.1) | copy-start | bytes 4718596
  2.2 1.4 %copy-start.3 = (bf16[8,48,2048]{2,1,0:T(8,128)(2,1)S(1)}, bf16[8,48,2048]{2,1,0:T(8,128)(2,1)}, u32[]{:S(2)}) copy-start(bf16[8,48,2048]{2,1,0:T(8,128)(2,1)} %nk_ref.1) | copy-start | bytes 4718596
  3.6 0.7 copy-start.5
  4.3 0.7 copy-start.8
  4.9 9.3 %copy-start.4 = (bf16[64,2048]{1,0:T(8,128)(2,1)S(1)}, bf16[64,2048]{1,0:T(8,128)(2,1)}, u32[]{:S(2)}) copy-start(bf16[64,2048]{1,0:T(8,128)(2,1)} %w_ref.2) | copy-start | bytes 786436
  14.3 1.4 %copy-start.1 = (bf16[8,48,2176]{2,1,0:T(8,128)(2,1)S(1)}, bf16[8,48,2176]{2,1,0:T(8,128)(2,1)}, u32[]{:S(2)}) copy-start(bf16[8,48,2176]{2,1,0:T(8,128)(2,1)} %attention_part.1.part) | copy-start | bytes 5013508
  15.7 76.1 %copy-start.6 = (s32[8,48]{1,0:T(8,128)S(1)}, s32[8,48]{1,0:T(8,128)}, u32[]{:S(2)}) copy-start(s32[8,48]{1,0:T(8,128)} %par_ref.1) | copy-start | bytes 4612
  15.7 76.1 %copy-start.9 = (s32[8,48]{1,0:T(8,128)S(1)}, s32[8,48]{1,0:T(8,128)}, u32[]{:S(2)}) copy-start(s32[8,48]{1,0:T(8,128)} %param.19) | copy-start | bytes 4612
  15.7 76.7 %copy-start.7 = (f32[2048]{0:T(1024)S(1)}, f32[2048]{0:T(1024)}, u32[]{:S(2)}) copy-start(f32[2048]{0:T(1024)} %param.22) | copy-start | bytes 24580

commit v3 on v2

--- a/solution.py
+++ b/solution.py
@@ -12,7 +12,7 @@
 F32 = jnp.float32
 BF16 = jnp.bfloat16
 MESH = pl.DeviceIdType.MESH
-VMEM_LIMIT = 50 * 1024 * 1024
+VMEM_LIMIT = 60 * 1024 * 1024
 
 
 def ancestor_mask(parents):
@@ -163,23 +163,23 @@
         when(self.z > 0, lambda: self.left(0).start())
         self.pair(self.z).start()
 
-    def forward(self):
+    def forward(self, k):
         z, chips = self.z, self.chips
-        for k in range(1, chips):
-
-            @pl.when(z - k >= 0)
-            def _():
-                self.right(k).wait_recv()
-                when(z < chips - 1, lambda: self.right(k).start())
-                self.pair(z - k).start()
-
-            @pl.when(z + k <= chips - 1)
-            def _():
-                self.left(k).wait_recv()
-                when(z > 0, lambda: self.left(k).start())
-                self.pair(z + k).start()
-
-        for zs in range(chips):
+
+        @pl.when(z - k >= 0)
+        def _():
+            self.right(k).wait_recv()
+            when(z < chips - 1, lambda: self.right(k).start())
+            self.pair(z - k).start()
+
+        @pl.when(z + k <= chips - 1)
+        def _():
+            self.left(k).wait_recv()
+            when(z > 0, lambda: self.left(k).start())
+            self.pair(z + k).start()
+
+    def arrive(self):
+        for zs in range(self.chips):
             self.copy(2 * zs + 1 - self.c, self.sends[2].at[zs], self.sib).wait_recv()
 
     def finish(self):
@@ -296,11 +296,10 @@
 
         pass_on(i, zd, buf, sems, to).start()
 
-    def sums(i):
-        for k in range(chips - 1):
-            rd, ld = chips - 1 - k, k
-            when(rd > z, functools.partial(step, i, rd, from_l, fl_r, z == 0, me + 2))
-            when(ld < z, functools.partial(step, i, ld, from_r, fr_r, z == chips - 1, me - 2))
+    def sums(i, k):
+        rd, ld = chips - 1 - k, k
+        when(rd > z, functools.partial(step, i, rd, from_l, fl_r, z == 0, me + 2))
+        when(ld < z, functools.partial(step, i, ld, from_r, fr_r, z == chips - 1, me - 2))
 
     first = [
         Line(chips, lambda j, i=i: att.at[j, rows(i)], g1_r.at[i], g1_a.at[i], g1_b.at[i], g1_c.at[i])
@@ -331,7 +330,7 @@
         first[i].start()
 
     def project(i):
-        first[i].forward()
+        first[i].arrive()
         if i == 0:
             for k in range(1, groups):
                 w_dp(k, lax.rem(grp + groups - k, groups)).wait_recv()
@@ -345,34 +344,36 @@
         second[i].start()
 
     def place(i):
-        second[i].forward()
+        second[i].arrive()
         for j in range(shards):
             for t in range(shards):
                 out_ref[t, rows(i), j * ncol : (j + 1) * ncol] = hcol[
                     j, i, t * CHUNK : (t + 1) * CHUNK
                 ]
 
-    sums(0)
-    for k in range(1, shards):
-        w_mp(k).start()
+    for k in range(chips - 1):
+        for i in range(chunks):
+            sums(i, k)
+        if k == 0:
+            for n in range(1, shards):
+                w_mp(n).start()
     for i in range(chunks):
-        if i + 1 < chunks:
-            sums(i + 1)
         attended(i)
-        if i == 0:
-            for k in range(1, shards):
-                w_mp(k).wait_recv()
-            own_w.wait()
-            for k in range(1, groups):
-                w_dp(k, grp).start()
-        if i >= 1:
-            project(i - 1)
-        if i >= 2:
-            place(i - 2)
-    project(chunks - 1)
-    if chunks >= 2:
-        place(chunks - 2)
-    place(chunks - 1)
+    for n in range(1, shards):
+        w_mp(n).wait_recv()
+    own_w.wait()
+    for n in range(1, groups):
+        w_dp(n, grp).start()
+    for k in range(1, chips):
+        for i in range(chunks):
+            first[i].forward(k)
+    for i in range(chunks):
+        project(i)
+    for k in range(1, chips):
+        for i in range(chunks):
+            second[i].forward(k)
+    for i in range(chunks):
+        place(i)
 
     for i in range(chunks):
         first[i].finish()

time: 108 us -> 99.3 us (0.919)
  Pallas kernels: 98.8 us -> 92.8 us
  local copies, waits for them, and re-layouts: 7.8 us -> 4.3 us
    pallas_call x1, Pallas kernels: 76.1 us -> 68.8 us  [hidden_of(): pl.pallas_call(functools.partial(hidden_kernel, chips, groups), in_specs=...]
    unnamed x21 -> x9, local copies, waits for them, and re-layouts: 6.87 us -> 1.16 us
where the time goes in v3:
time: 99.3 us; the launch traced here: 98.6 us
  Pallas kernels  92.8 us (93%)
  local copies, waits for them, and re-layouts  4.3 us (4%)
    pallas_call x1, Pallas kernels, hidden_of(): pl.pallas_call(functools.partial(hidden_kernel, chips, groups), in_specs=...  68.8 us
    pallas_call x1, Pallas kernels, score(): pl.pallas_call(functools.partial(score_kernel, vocab, shards), grid=(pl.c...  13.9 us
    pallas_call x1, Pallas kernels, attention(): pl.pallas_call(functools.partial(attention_kernel, shards), grid=(reqs,),...  10.1 us

profile of v3, /device:TPU:0, one launch (start us, length us, event | category | flops | bytes accessed | tf_op | source)
XLA Modules:
  0.0 98.6 jit_solution(4607130085520276978)
XLA Ops:
  0.6 0.0 copy-start
  0.6 10.1 %attention_part.1.part = bf16[8,48,2176]{2,1,0:T(8,128)(2,1)} custom-call(s32[8]{0:T(128)} %len_ref.1, bf16[8,48,2048]{2,1,0:T(8,128)(2,1)} %q_ref.1, bf16[8,128,2048]{2,1,0:T(8,128)(2,1)} %k_ref.1, bf16[8,128,2048]{2,1,0:T(8,128)(2,1)} %v_ref.1, bf16[8,48,2048]{2,1,0:T(8,128)(2,1)} %nk_ref.1, bf16[8,48,2048]{2,1,0:T(8,128)(2,1)} %nv_ref.1, s32[8,48]{1,0:T(8,128)} %par_ref.1), custom_call_target="tpu_custom_call" | custom-call | tf_op jit(solution)/shard_map/attention_part/pallas_call | solution.py:114
  10.7 0.0 copy-done
  10.7 0.7 constant_dynamic-slice_fusion
  11.4 0.0 copy-start.2
  11.4 0.0 copy-start.3
  11.4 68.8 %hidden_exchange.1 = bf16[8,48,2048]{2,1,0:T(8,128)(2,1)} custom-call(bf16[8,48,2176]{2,1,0:T(8,128)(2,1)} %attention_part.1.part, bf16[64,2048]{1,0:T(8,128)(2,1)} %w_ref.2, bf16[8,48,256]{2,1,0:T(8,128)(2,1)} %bitcast.10), custom_call_target="tpu_custom_call" | custom-call | tf_op jit(solution)/shard_map/hidden_exchange/pallas_call | solution.py:399
  80.3 0.0 copy-done.2
  80.3 0.0 copy-done.3
  80.3 0.1 stack.14
  80.4 0.1 slice.35
  80.5 0.1 stack.13
  80.6 0.1 slice.34
  80.7 0.1 stack.12
  80.8 0.1 copy.17
  80.9 0.7 pad.28.t_ref
  81.6 0.0 copy-start.1
  81.6 13.9 %score_exchange.1 = f32[8,384]{1,0:T(8,128)} custom-call(bf16[384,2048]{1,0:T(8,128)(2,1)} %bitcast.9, f32[1,2048]{1,0:T(1,128)} %bitcast.15, s32[384,128]{1,0:T(8,128)} %pad.28.t_ref, bf16[2048,2432]{1,0:T(8,128)(2,1)} %w_ref.3), custom_call_target="tpu_custom_call" | custom-call | tf_op jit(solution)/shard_map/score_exchange/pallas_call | solution.py:488
  95.5 0.9 slice_reduce_fusion.2
  96.4 0.1 squeeze.15
  96.5 0.1 squeeze.12
  96.6 0.1 squeeze.14
  96.7 0.1 squeeze.13
  96.7 0.7 log_subtract_fusion
  97.4 0.0 copy-done.1
  97.4 1.1 %copy.19 = bf16[8,48,2048]{2,1,0:T(8,128)(2,1)} copy(bf16[8,48,2048]{2,1,0:T(8,128)(2,1)S(1)} %copy-done.1) | data formatting | bytes 3145728
  (7 shorter events, 0.1 us)
Async XLA Ops:
  0.6 10.1 %copy-start = (bf16[8,48,2048]{2,1,0:T(8,128)(2,1)S(1)}, bf16[8,48,2048]{2,1,0:T(8,128)(2,1)}, u32[]{:S(2)}) copy-start(bf16[8,48,2048]{2,1,0:T(8,128)(2,1)} %param.20) | copy-start | bytes 4718596
  11.4 68.9 %copy-start.2 = (s32[8,48]{1,0:T(8,128)S(1)}, s32[8,48]{1,0:T(8,128)}, u32[]{:S(2)}) copy-start(s32[8,48]{1,0:T(8,128)} %par_ref.1) | copy-start | bytes 4612
  11.4 68.9 %copy-start.3 = (s32[8,48]{1,0:T(8,128)S(1)}, s32[8,48]{1,0:T(8,128)}, u32[]{:S(2)}) copy-start(s32[8,48]{1,0:T(8,128)} %param.19) | copy-start | bytes 4612
  81.6 15.8 %copy-start.1 = (bf16[8,48,2048]{2,1,0:T(8,128)(2,1)S(1)}, bf16[8,48,2048]{2,1,0:T(8,128)(2,1)}, u32[]{:S(2)}) copy-start(bf16[8,48,2048]{2,1,0:T(8,128)(2,1)} %hidden_exchange.1) | copy-start | bytes 4718596

commit v4 on v3

--- a/solution.py
+++ b/solution.py
@@ -195,10 +195,10 @@
 
 
 def hidden_kernel(
-    chips, groups, part, w_ref, res_ref, out_ref,
+    chips, groups, part, w_ref, res_ref, gain_ref, mark_ref, vocab_ref, out_ref, stat_ref,
     own_buf, sib_buf, from_l, from_r, acc, tot, att, wcol, hcol,
     own_s, sib_s, sib_r, fl_r, fr_r, acc_s, g1_r, g1_a, g1_b, g1_c, g2_r, g2_a, g2_b, g2_c,
-    w1_s, w1_r, w2_s, w2_r, wown_s,
+    w1_s, w1_r, w2_s, w2_r, wown_s, vbuf, stats, slots, t_s, t_r, v_s,
 ):
     shards = 2 * chips
     me = lax.axis_index("mp")
@@ -242,6 +242,8 @@
             mine(i, zd).start()
     own_w = pltpu.make_async_copy(w_ref.at[:, columns(me)], wcol.at[grp, me], wown_s)
     own_w.start()
+    load_vocab = pltpu.make_async_copy(vocab_ref, vbuf, v_s)
+    load_vocab.start()
 
     pl.semaphore_wait(barrier, shards - 1 + groups - 1)
 
@@ -343,6 +345,38 @@
         hcol[me, i] = (res.astype(F32) + projected).astype(BF16)
         second[i].start()
 
+    def total_copy(i, n):
+        return pltpu.make_async_remote_copy(
+            src_ref=stats.at[i], dst_ref=slots.at[n, i], send_sem=t_s.at[i, n],
+            recv_sem=t_r.at[i, n], device_id={"mp": lax.rem(me + n, shards)}, device_id_type=MESH,
+        )
+
+    def score(i):
+        count = shards * CHUNK
+        h = out_ref[:, rows(i), :].reshape(count, width).astype(F32)
+        normed = (
+            h * lax.rsqrt(jnp.mean(h * h, -1, keepdims=True) + 1e-06) * gain_ref[...]
+        ).astype(BF16)
+        lane = lax.broadcasted_iota(jnp.int32, (count, 128), 1)
+        mark = mark_ref[:, rows(i), :].reshape(count, 128)
+        marks = [mark[:, n : n + 1] for n in range(3)]
+        new = [jnp.zeros((count, 128), F32) for _ in range(4)]
+        vocab = vbuf.shape[1]
+        for low in range(0, vocab, 512):
+            high = min(low + 512, vocab)
+            logits = jnp.dot(normed, vbuf[:, low:high], preferred_element_type=F32)
+            for b in range(0, high - low, 128):
+                x = logits[:, b : b + 128]
+                new[0] += jnp.exp(x)
+                for n in range(3):
+                    new[n + 1] += jnp.where(lane + (low + b) == marks[n], x, 0.0)
+        stat = jnp.zeros((count, 128), F32)
+        for n in range(4):
+            stat = jnp.where(lane == n, jnp.sum(new[n], -1, keepdims=True), stat)
+        stats[i] = jnp.transpose(stat)[:8]
+        for n in range(1, shards):
+            total_copy(i, n).start()
+
     def place(i):
         second[i].arrive()
         for j in range(shards):
@@ -369,11 +403,21 @@
             first[i].forward(k)
     for i in range(chunks):
         project(i)
-    for k in range(1, chips):
+    for k in range(1, chips - 1):
         for i in range(chunks):
             second[i].forward(k)
     for i in range(chunks):
+        second[i].forward(chips - 1)
         place(i)
+        if i == 0:
+            load_vocab.wait()
+        score(i)
+    for i in range(chunks):
+        total = stats[i]
+        for n in range(1, shards):
+            total_copy(i, n).wait_recv()
+            total = total + slots[n, i]
+        stat_ref[i] = total
 
     for i in range(chunks):
         first[i].finish()
@@ -385,22 +429,29 @@
         w_mp(k).wait_send()
     for k in range(1, groups):
         w_dp(k, grp).wait_send()
-
-
-def hidden_of(shards, groups, part, out_weight, res):
+    for i in range(chunks):
+        for n in range(1, shards):
+            total_copy(i, n).wait_send()
+
+
+def hidden_of(shards, groups, part, out_weight, res, gain, marks, vocab_weight):
     own, width = part.shape[1], out_weight.shape[1]
     wide = part.shape[2]
     ncol = width // shards
     chips = shards // 2
     chunks = own // CHUNK
     dma = pltpu.SemaphoreType.DMA
+    anywhere = pl.BlockSpec(memory_space=pl.ANY)
     gather_sems = [dma((chunks, shards))] + [dma((chunks, chips))] * 3
     vmem = pl.BlockSpec(memory_space=pltpu.VMEM)
     return pl.pallas_call(
         functools.partial(hidden_kernel, chips, groups),
-        in_specs=[pl.BlockSpec(memory_space=pl.ANY), vmem, vmem],
-        out_specs=vmem,
-        out_shape=jax.ShapeDtypeStruct((shards, own, width), BF16),
+        in_specs=[anywhere, vmem, vmem, vmem, vmem, anywhere],
+        out_specs=[vmem, vmem],
+        out_shape=[
+            jax.ShapeDtypeStruct((shards, own, width), BF16),
+            jax.ShapeDtypeStruct((chunks, 8, shards * CHUNK), F32),
+        ],
         scratch_shapes=[
             pltpu.VMEM((chips, own, wide), BF16),
             pltpu.VMEM((chips, own, wide), BF16),
@@ -415,100 +466,16 @@
             *gather_sems,
             *gather_sems,
             dma((shards,)), dma((shards,)), dma((groups,)), dma((groups,)), dma,
+            pltpu.VMEM(vocab_weight.shape, BF16),
+            pltpu.VMEM((chunks, 8, shards * CHUNK), F32),
+            pltpu.VMEM((shards, chunks, 8, shards * CHUNK), F32),
+            dma((chunks, shards)), dma((chunks, shards)), dma,
         ],
         compiler_params=pltpu.CompilerParams(
             collective_id=0, has_side_effects=True, vmem_limit_bytes=VMEM_LIMIT
         ),
         name="hidden_exchange",
-    )(part, out_weight, res)
-
-
-def score_kernel(vocab, shards, h_ref, g_ref, t_ref, w_ref, o_ref, normed, sums, stats, slots, send, recv):
-    step = pl.program_id(0)
-    tile = w_ref.shape[1]
-    rows = h_ref.shape[0]
-    me = lax.axis_index("mp")
-    barrier = pltpu.get_barrier_semaphore()
-
-    @pl.when(step == 0)
-    def _():
-        for k in range(1, shards):
-            pl.semaphore_signal(
-                barrier, inc=1, device_id={"mp": lax.rem(me + k, shards)}, device_id_type=MESH
-            )
-        h = h_ref[...].astype(F32)
-        normed[...] = (
-            h * lax.rsqrt(jnp.mean(h * h, -1, keepdims=True) + 1e-06) * g_ref[...]
-        ).astype(BF16)
-        sums[...] = jnp.zeros_like(sums)
-
-    logits = jnp.dot(normed[...], w_ref[...], preferred_element_type=F32)
-    lane = lax.broadcasted_iota(jnp.int32, (rows, 128), 1)
-    marks = [t_ref[:, n : n + 1] for n in range(3)]
-    new = [jnp.zeros((rows, 128), F32) for _ in range(4)]
-    for b in range(tile // 128):
-        col = step * tile + b * 128 + lane
-        x = logits[:, b * 128 : (b + 1) * 128]
-        new[0] += jnp.where(col < vocab, jnp.exp(x), 0.0)
-        for n in range(3):
-            new[n + 1] += jnp.where(col == marks[n], x, 0.0)
-    for n in range(4):
-        sums[n] += new[n]
-
-    @pl.when(step == pl.num_programs(0) - 1)
-    def _():
-        stat = jnp.zeros((rows, 128), F32)
-        for n in range(4):
-            stat = jnp.where(lane == n, jnp.sum(sums[n], -1, keepdims=True), stat)
-        stats[...] = jnp.transpose(stat)[:8]
-        pl.semaphore_wait(barrier, shards - 1)
-
-        def copy(k):
-            return pltpu.make_async_remote_copy(
-                src_ref=stats, dst_ref=slots.at[k], send_sem=send.at[k], recv_sem=recv.at[k],
-                device_id={"mp": lax.rem(me + k, shards)}, device_id_type=MESH,
-            )
-
-        for k in range(1, shards):
-            copy(k).start()
-        total = stats[...]
-        for k in range(1, shards):
-            copy(k).wait_recv()
-            total = total + slots[k]
-        o_ref[...] = total
-        for k in range(1, shards):
-            copy(k).wait_send()
-
-
-def score(shards, hidden, gain, marks, vocab_weight):
-    rows, width = hidden.shape
-    vocab = vocab_weight.shape[1]
-    tile = 512
-    dma = pltpu.SemaphoreType.DMA
-    return pl.pallas_call(
-        functools.partial(score_kernel, vocab, shards),
-        grid=(pl.cdiv(vocab, tile),),
-        in_specs=[
-            pl.BlockSpec((rows, width), lambda i: (0, 0)),
-            pl.BlockSpec((1, width), lambda i: (0, 0)),
-            pl.BlockSpec((rows, 128), lambda i: (0, 0)),
-            pl.BlockSpec((width, tile), lambda i: (0, i)),
-        ],
-        out_specs=pl.BlockSpec((8, rows), lambda i: (0, 0)),
-        out_shape=jax.ShapeDtypeStruct((8, rows), F32),
-        scratch_shapes=[
-            pltpu.VMEM((rows, width), BF16),
-            pltpu.VMEM((4, rows, 128), F32),
-            pltpu.VMEM((8, rows), F32),
-            pltpu.VMEM((shards, 8, rows), F32),
-            dma((shards,)),
-            dma((shards,)),
-        ],
-        compiler_params=pltpu.CompilerParams(
-            collective_id=1, has_side_effects=True, vmem_limit_bytes=VMEM_LIMIT
-        ),
-        name="score_exchange",
-    )(hidden, gain, marks, vocab_weight)
+    )(part, out_weight, res, gain, marks, vocab_weight)
 
 
 def local_fast(
@@ -526,8 +493,6 @@
     ).reshape(shards, tokens // shards, width + 128)
     res = lax.dynamic_slice_in_dim(residual.reshape(tokens, width), shard * ncol, ncol, 1)
     res = res.reshape(shards, tokens // shards, ncol)
-    hidden = hidden_of(shards, groups, part, out_weight, res).reshape(tokens, width)
-
     vocab = vocab_weight.shape[1]
     column = tree_tokens - shard * vocab
     column = jnp.where((column >= 0) & (column < vocab), column, -1)
@@ -543,8 +508,13 @@
         [ahead(jnp.where(by_one, column, -1), 1), ahead(jnp.where(by_two, column, -1), 2), first], -1
     ).reshape(tokens, 3)
     marks = jnp.pad(marks, ((0, 0), (0, 125)), constant_values=-1)
-    stats = score(shards, hidden, norm_gain.reshape(1, width), marks, vocab_weight)
-    total = stats.reshape(8, reqs, tree)
+    own = tokens // shards
+    hidden, stats = hidden_of(
+        shards, groups, part, out_weight, res, norm_gain.reshape(1, width),
+        marks.reshape(shards, own, 128), vocab_weight,
+    )
+    total = stats.reshape(own // CHUNK, 8, shards, CHUNK).transpose(1, 2, 0, 3)
+    total = total.reshape(8, reqs, tree)
 
     def behind(x, n):
         return jnp.pad(x[:, : tree - n], ((0, 0), (n, 0)))
@@ -642,6 +612,7 @@
         and width % (shards * 128) == 0
         and width == HEADS * 128
         and tree % 16 == 0
+        and vocab_weight.shape[1] % 128 == 0
         and shards % 2 == 0
         and shards >= 8
     )

time: 99.3 us -> 99.2 us (level)
  Pallas kernels: 92.8 us -> 89.5 us
  local copies, waits for them, and re-layouts: 4.3 us -> 7.26 us
    pallas_call x1 -> x0, Pallas kernels: 13.9 us -> none  [score(): pl.pallas_call(functools.partial(score_kernel, vocab, shards), grid=(pl.c...]
    pallas_call x1, Pallas kernels: 68.8 us -> 79.6 us  [hidden_of(): pl.pallas_call(functools.partial(hidden_kernel, chips, groups), in_specs=...]
    unnamed x9 -> x4, local copies, waits for them, and re-layouts: 1.16 us -> 4.27 us
where the time goes in v4:
time: 99.2 us; the launch traced here: 98.9 us
  Pallas kernels  89.5 us (90%)
  local copies, waits for them, and re-layouts  7.26 us (7%)
  other arithmetic  1.43 us (1%)
    pallas_call x1, Pallas kernels, hidden_of(): pl.pallas_call(functools.partial(hidden_kernel, chips, groups), in_specs=...  79.6 us
    pallas_call x1, Pallas kernels, attention(): pl.pallas_call(functools.partial(attention_kernel, shards), grid=(reqs,),...  9.92 us
    unnamed x4, local copies, waits for them, and re-layouts  4.27 us

profile of v4, /device:TPU:0, one launch (start us, length us, event | category | flops | bytes accessed | tf_op | source)
XLA Modules:
  0.0 98.9 jit_solution(17222838462326275380)
XLA Ops:
  0.6 0.0 copy-start
  0.6 1.4 %copy-done = bf16[8,48,2048]{2,1,0:T(8,128)(2,1)S(1)} copy-done((bf16[8,48,2048]{2,1,0:T(8,128)(2,1)S(1)}, bf16[8,48,2048]{2,1,0:T(8,128)(2,1)}, u32[]{:S(2)}) %copy-start) | copy-done | bytes 1572888
  2.1 0.7 broadcast_select_fusion.1
  2.8 0.1 slice.34
  2.9 0.1 stack.12
  2.9 0.1 stack.14
  3.0 0.1 slice.35
  3.1 0.1 stack.13
  3.2 0.1 copy.27
  3.4 0.7 pad.28.clone
  4.0 0.7 constant_dynamic-slice_fusion
  4.8 9.9 %attention_part.1.part = bf16[8,48,2176]{2,1,0:T(8,128)(2,1)} custom-call(s32[8]{0:T(128)} %len_ref.1, bf16[8,48,2048]{2,1,0:T(8,128)(2,1)} %q_ref.1, bf16[8,128,2048]{2,1,0:T(8,128)(2,1)} %k_ref.1, bf16[8,128,2048]{2,1,0:T(8,128)(2,1)} %v_ref.1, bf16[8,48,2048]{2,1,0:T(8,128)(2,1)} %nk_ref.1, bf16[8,48,2048]{2,1,0:T(8,128)(2,1)} %nv_ref.1, s32[8,48]{1,0:T(8,128)} %par_ref.1), custom_call_target="tpu_custom_call" | custom-call | tf_op jit(solution)/shard_map/attention_part/pallas_call | solution.py:114
  14.7 79.6 %hidden_exchange.1 = (bf16[8,48,2048]{2,1,0:T(8,128)(2,1)}, f32[3,8,128]{2,1,0:T(8,128)}) custom-call(bf16[8,48,2176]{2,1,0:T(8,128)(2,1)} %attention_part.1.part, bf16[64,2048]{1,0:T(8,128)(2,1)} %w_ref.1, bf16[8,48,256]{2,1,0:T(8,128)(2,1)} %bitcast.13, f32[1,2048]{1,0:T(1,128)} %bitcast.19, s32[8,48,128]{2,1,0:T(8,128)} %bitcast.12, ...), custom_call_target="tpu_custom_call" | custom-call | tf_op jit(solution)/shard_map/hidden_exchange/pallas_call | solution.py:447
  94.3 0.8 reshape.64
  95.1 0.1 copy.29
  95.2 0.1 squeeze.13
  95.3 0.1 squeeze.15
  95.4 0.1 squeeze.14
  95.4 0.1 squeeze.12
  95.5 0.7 log_subtract_fusion
  96.2 2.7 %copy.31 = bf16[8,48,2048]{2,1,0:T(8,128)(2,1)} copy(bf16[8,48,2048]{2,1,0:T(8,128)(2,1)} %get-tuple-element.20) | data formatting | bytes 3145728
  (7 shorter events, 0.1 us)
Async XLA Ops:
  0.6 1.4 %copy-start = (bf16[8,48,2048]{2,1,0:T(8,128)(2,1)S(1)}, bf16[8,48,2048]{2,1,0:T(8,128)(2,1)}, u32[]{:S(2)}) copy-start(bf16[8,48,2048]{2,1,0:T(8,128)(2,1)} %param.20) | copy-start | bytes 4718596

commit v5 on v4

--- a/solution.py
+++ b/solution.py
@@ -12,7 +12,7 @@
 F32 = jnp.float32
 BF16 = jnp.bfloat16
 MESH = pl.DeviceIdType.MESH
-VMEM_LIMIT = 60 * 1024 * 1024
+VMEM_LIMIT = 56 * 1024 * 1024
 
 
 def ancestor_mask(parents):
@@ -28,107 +28,53 @@
     return links > 0.5
 
 
-def attention_kernel(
-    shards, len_ref, q_ref, k_ref, v_ref, nk_ref, nv_ref, par_ref, o_ref, chain
-):
-    req = pl.program_id(0)
-    shard = lax.axis_index("mp")
-    slots = k_ref.shape[1]
+def attend(q_ref, keys, values, mask, o_ref, req):
     tree, width = q_ref.shape[1:]
-    reqs = par_ref.shape[0]
     hd = width // HEADS
     scale = hd ** (-0.5)
-    cap = slots * shards
-    length = len_ref[req]
-    start = shard * slots
-    tree_shard = max(shards // 8, 1)
-    seen = (start < length) & ((start < SINK) | (start + slots > length - cap // 2))
-
-    def attend(keys, values, mask):
-        lane = lax.broadcasted_iota(jnp.int32, (tree, 128), 1)
-        low = lax.broadcasted_iota(jnp.int32, (tree, 2 * hd), 1) < hd
-        mask2 = jnp.concatenate([mask, mask], 0)
-        den = jnp.zeros((tree, 128), F32)
-        pairs = HEADS // 2
-        for group in range(0, pairs, 4):
-            scores = []
-            for p in range(group, group + 4):
-                cols = slice(2 * p * hd, 2 * (p + 1) * hd)
-                q = q_ref[0, :, cols]
-                both = jnp.concatenate(
-                    [jnp.where(low, q, jnp.zeros_like(q)), jnp.where(low, jnp.zeros_like(q), q)], 0
+    lane = lax.broadcasted_iota(jnp.int32, (tree, 128), 1)
+    low = lax.broadcasted_iota(jnp.int32, (tree, 2 * hd), 1) < hd
+    mask2 = jnp.concatenate([mask, mask], 0)
+    den = jnp.zeros((tree, 128), F32)
+    pairs = HEADS // 2
+    for group in range(0, pairs, 4):
+        scores = []
+        for p in range(group, group + 4):
+            cols = slice(2 * p * hd, 2 * (p + 1) * hd)
+            q = q_ref[req, :, cols]
+            both = jnp.concatenate(
+                [jnp.where(low, q, jnp.zeros_like(q)), jnp.where(low, jnp.zeros_like(q), q)], 0
+            )
+            scores.append(
+                lax.dot_general(
+                    both, keys[req, :, cols], (((1,), (1,)), ((), ())),
+                    preferred_element_type=F32,
                 )
-                scores.append(
-                    lax.dot_general(
-                        both, keys[0, :, cols], (((1,), (1,)), ((), ())),
-                        preferred_element_type=F32,
-                    )
-                )
-            es = [jnp.where(mask2 > 0.5, jnp.exp(s * scale), 0.0) for s in scores]
-            for n, e in enumerate(es):
-                p = group + n
-                cols = slice(2 * p * hd, 2 * (p + 1) * hd)
-                num = jnp.dot(e.astype(BF16), values[0, :, cols], preferred_element_type=F32)
-                o_ref[0, :, 2 * p * hd : (2 * p + 1) * hd] = num[:tree, :hd].astype(BF16)
-                o_ref[0, :, (2 * p + 1) * hd : 2 * (p + 1) * hd] = num[tree:, hd:].astype(BF16)
-                d = jnp.sum(e, -1, keepdims=True)
-                den = jnp.where(lane == 2 * p, d[:tree], den)
-                den = jnp.where(lane == 2 * p + 1, d[tree:], den)
-        o_ref[0, :, width:] = den.astype(BF16)
-
-    @pl.when((shard == tree_shard) & (req == 0))
-    def _():
-        node = lax.broadcasted_iota(jnp.int32, (reqs, 128), 1)
-        rows = []
-        for j in range(tree):
-            row = jnp.where(node == j, 1.0, 0.0)
-            if j == 1:
-                row = row + rows[0]
-            elif j > 1:
-                row = row + jnp.where(par_ref[:, j : j + 1] == j - 1, rows[j - 1], rows[j - 2])
-            rows.append(row)
-            chain[j] = row
-
-    @pl.when(shard == tree_shard)
-    def _():
-        attend(nk_ref, nv_ref, chain[:, req, :][:, :tree])
-
-    @pl.when((shard != tree_shard) & seen)
-    def _():
-        pos = start + lax.broadcasted_iota(jnp.int32, (tree, slots), 1)
-        mask = (pos < length) & ((pos < SINK) | (pos >= length - cap // 2))
-        attend(k_ref, v_ref, jnp.where(mask, 1.0, 0.0))
-
-    @pl.when((shard != tree_shard) & jnp.logical_not(seen))
-    def _():
-        o_ref[...] = jnp.zeros_like(o_ref)
-
-
-def attention(shards, queries, new_keys, new_values, cache_keys, cache_values, lengths, parents):
-    reqs, tree, width = queries.shape
-    slots = cache_keys.shape[1]
-
-    def block(rows, cols):
-        return pl.BlockSpec((1, rows, cols), lambda r: (r, 0, 0))
-
-    return pl.pallas_call(
-        functools.partial(attention_kernel, shards),
-        grid=(reqs,),
-        in_specs=[
-            pl.BlockSpec(memory_space=pltpu.SMEM),
-            block(tree, width),
-            block(slots, width),
-            block(slots, width),
-            block(tree, width),
-            block(tree, width),
-            pl.BlockSpec((reqs, tree), lambda r: (0, 0)),
-        ],
-        out_specs=block(tree, width + 128),
-        out_shape=jax.ShapeDtypeStruct((reqs, tree, width + 128), BF16),
-        scratch_shapes=[pltpu.VMEM((tree, reqs, 128), F32)],
-        compiler_params=pltpu.CompilerParams(vmem_limit_bytes=VMEM_LIMIT),
-        name="attention_part",
-    )(lengths, queries, cache_keys, cache_values, new_keys, new_values, parents)
+            )
+        es = [jnp.where(mask2 > 0.5, jnp.exp(s * scale), 0.0) for s in scores]
+        for n, e in enumerate(es):
+            p = group + n
+            cols = slice(2 * p * hd, 2 * (p + 1) * hd)
+            num = jnp.dot(e.astype(BF16), values[req, :, cols], preferred_element_type=F32)
+            o_ref[req, :, 2 * p * hd : (2 * p + 1) * hd] = num[:tree, :hd].astype(BF16)
+            o_ref[req, :, (2 * p + 1) * hd : 2 * (p + 1) * hd] = num[tree:, hd:].astype(BF16)
+            d = jnp.sum(e, -1, keepdims=True)
+            den = jnp.where(lane == 2 * p, d[:tree], den)
+            den = jnp.where(lane == 2 * p + 1, d[tree:], den)
+    o_ref[req, :, width:] = den.astype(BF16)
+
+
+def ancestors(par, chain):
+    node = lax.broadcasted_iota(jnp.int32, (par.shape[0], 128), 1)
+    rows = []
+    for j in range(par.shape[1]):
+        row = jnp.where(node == j, 1.0, 0.0)
+        if j == 1:
+            row = row + rows[0]
+        elif j > 1:
+            row = row + jnp.where(par[:, j : j + 1] == j - 1, rows[j - 1], rows[j - 2])
+        rows.append(row)
+        chain[j] = row
 
 
 def when(cond, fn):
@@ -195,9 +141,12 @@
 
 
 def hidden_kernel(
-    chips, groups, part, w_ref, res_ref, gain_ref, mark_ref, vocab_ref, out_ref, stat_ref,
-    own_buf, sib_buf, from_l, from_r, acc, tot, att, wcol, hcol,
-    own_s, sib_s, sib_r, fl_r, fr_r, acc_s, g1_r, g1_a, g1_b, g1_c, g2_r, g2_a, g2_b, g2_c,
+    chips, groups, len_ref, q_hbm, k_hbm, v_hbm, nk_hbm, nv_hbm, par_hbm, tok_hbm, res_hbm,
+    w_ref, gain_ref, vocab_ref, out_ref, stat_ref,
+    q_ref, k_ref, v_ref, nk_ref, nv_ref, par_ref, tok_ref, res_ref, chain, mark, part,
+    q_s, k_s, v_s0, par_s, tok_s, res_s,
+    sib_buf, from_l, from_r, acc, tot, att, wcol, hcol,
+    sib_s, sib_r, fl_r, fr_r, acc_s, g1_r, g1_a, g1_b, g1_c, g2_r, g2_a, g2_b, g2_c,
     w1_s, w1_r, w2_s, w2_r, wown_s, vbuf, stats, slots, t_s, t_r, v_s,
 ):
     shards = 2 * chips
@@ -206,15 +155,35 @@
     c, z = lax.rem(me, 2), lax.div(me, 2)
     sib = 2 * z + 1 - c
     width = att.shape[-1]
+    tree = q_ref.shape[1]
+    span = k_ref.shape[1]
+    cap = span * shards
     hd = width // HEADS
     ncol = wcol.shape[-1]
+    vocab = vbuf.shape[1]
     chunks = att.shape[1] // CHUNK
+    tree_shard = max(shards // 8, 1)
+    on_tree = me == tree_shard
+    on_cache = (me < tree_shard) | (me >= shards // 2)
 
     def rows(i):
         return pl.ds(i * CHUNK, CHUNK)
 
     def columns(j):
         return pl.ds(pl.multiple_of(j * ncol, 128), ncol)
+
+    def loads(r, keys, key_buf, values, value_buf):
+        return [
+            pltpu.make_async_copy(q_hbm.at[r], q_ref.at[r], q_s.at[r]),
+            pltpu.make_async_copy(keys.at[r], key_buf.at[r], k_s.at[r]),
+            pltpu.make_async_copy(values.at[r], value_buf.at[r], v_s0.at[r]),
+        ]
+
+    def cache_loads(r):
+        return loads(r, k_hbm, k_ref, v_hbm, v_ref)
+
+    def tree_loads(r):
+        return loads(r, nk_hbm, nk_ref, nv_hbm, nv_ref)
 
     barrier = pltpu.get_barrier_semaphore()
     for k in range(1, shards):
@@ -232,18 +201,33 @@
             if zd not in order:
                 order.append(zd)
 
-    def mine(i, zd):
-        return pltpu.make_async_copy(
-            part.at[2 * zd + c, rows(i)], own_buf.at[zd, rows(i)], own_s.at[i, zd]
-        )
-
-    for i in range(chunks):
-        for zd in order:
-            mine(i, zd).start()
+    load_par = pltpu.make_async_copy(par_hbm, par_ref, par_s)
+    load_tok = pltpu.make_async_copy(tok_hbm, tok_ref, tok_s)
+    load_par.start()
+    load_tok.start()
+    for zd in order:
+        for r in (2 * zd, 2 * zd + 1):
+            when(on_cache, lambda: [x.start() for x in cache_loads(r)] and None)
+            when(on_tree, lambda: [x.start() for x in tree_loads(r)] and None)
     own_w = pltpu.make_async_copy(w_ref.at[:, columns(me)], wcol.at[grp, me], wown_s)
     own_w.start()
+    load_res = pltpu.make_async_copy(res_hbm.at[:, :, columns(me)], res_ref, res_s)
+    load_res.start()
     load_vocab = pltpu.make_async_copy(vocab_ref, vbuf, v_s)
     load_vocab.start()
+
+    load_par.wait()
+    load_tok.wait()
+    when(on_tree, lambda: ancestors(par_ref[...], chain))
+
+    idx = lax.broadcasted_iota(jnp.int32, par_ref.shape, 1)
+    column = tok_ref[...] - me * vocab
+    column = jnp.where((column >= 0) & (column < vocab), column, -1)
+    mark[...] = jnp.full(mark.shape, -1.0, F32)
+    mark[0:8, 0:tree] = jnp.where((par_ref[...] == idx - 1) & (idx > 0), column, -1).astype(F32)
+    mark[8:16, 0:tree] = jnp.where((par_ref[...] == idx - 2) & (idx > 1), column, -1).astype(F32)
+    mark[16:24, 0:tree] = jnp.where(idx == 0, column, -1).astype(F32)
+    mark[...] = jnp.transpose(mark[...])
 
     pl.semaphore_wait(barrier, shards - 1 + groups - 1)
 
@@ -254,10 +238,6 @@
             device_id={"mp": sib}, device_id_type=MESH,
         )
 
-    for i in range(chunks):
-        for zd in order:
-            pair(i, zd).start()
-
     def w_mp(k):
         to = lax.rem(me + k, shards)
         return pltpu.make_async_remote_copy(
@@ -271,6 +251,48 @@
             recv_sem=w2_r.at[k], device_id={"dp": lax.rem(grp + k, groups)}, device_id_type=MESH,
         )
 
+    for n in range(1, shards):
+        w_mp(n).start()
+
+    def one_request(n, carry):
+        k = lax.div(n, 2)
+        zd = jnp.where(lax.rem(k, 2) == 0, chips - 1 - lax.div(k, 2), lax.div(k, 2))
+        r = 2 * zd + lax.rem(n, 2)
+
+        @pl.when(on_cache)
+        def _():
+            for x in cache_loads(r):
+                x.wait()
+            length = len_ref[r]
+            pos = me * span + lax.broadcasted_iota(jnp.int32, (tree, span), 1)
+            mask = (pos < length) & ((pos < SINK) | (pos >= length - cap // 2))
+            attend(q_ref, k_ref, v_ref, jnp.where(mask, 1.0, 0.0), part, r)
+
+        @pl.when(on_tree)
+        def _():
+            for x in tree_loads(r):
+                x.wait()
+            attend(q_ref, nk_ref, nv_ref, chain[:, r, :][:, :tree], part, r)
+
+        @pl.when(jnp.logical_not(on_cache | on_tree))
+        def _():
+            part[r] = jnp.zeros(part.shape[1:], BF16)
+
+        @pl.when(lax.rem(n, 2) != c)
+        def _():
+            for i in range(chunks):
+                pair(i, zd).start()
+
+        return carry
+
+    lax.fori_loop(0, shards, one_request, 0)
+
+    for n in range(1, shards):
+        w_mp(n).wait_recv()
+    own_w.wait()
+    for n in range(1, groups):
+        w_dp(n, grp).start()
+
     def pass_on(i, zd, buf, sems, to):
         return pltpu.make_async_remote_copy(
             src_ref=acc.at[zd, rows(i)], dst_ref=buf.at[zd, rows(i)], send_sem=acc_s.at[i, zd],
@@ -278,10 +300,9 @@
         )
 
     def both(i, zd):
-        return own_buf[zd, rows(i)].astype(F32) + sib_buf[zd, rows(i)].astype(F32)
+        return part[2 * zd + c, rows(i)].astype(F32) + sib_buf[zd, rows(i)].astype(F32)
 
     def arrive(i, zd):
-        mine(i, zd).wait()
         pair(i, zd).wait_recv()
 
     def step(i, zd, buf, sems, first, to):
@@ -334,6 +355,7 @@
     def project(i):
         first[i].arrive()
         if i == 0:
+            load_res.wait()
             for k in range(1, groups):
                 w_dp(k, lax.rem(grp + groups - k, groups)).wait_recv()
         projected = jnp.dot(
@@ -358,10 +380,15 @@
             h * lax.rsqrt(jnp.mean(h * h, -1, keepdims=True) + 1e-06) * gain_ref[...]
         ).astype(BF16)
         lane = lax.broadcasted_iota(jnp.int32, (count, 128), 1)
-        mark = mark_ref[:, rows(i), :].reshape(count, 128)
-        marks = [mark[:, n : n + 1] for n in range(3)]
+        marks = []
+        for n, ahead in enumerate((1, 2, 0)):
+            low = i * CHUNK + ahead
+            marks.append(
+                jnp.concatenate(
+                    [mark[low : low + CHUNK, 8 * n + t : 8 * n + t + 1] for t in range(shards)], 0
+                ).astype(jnp.int32)
+            )
         new = [jnp.zeros((count, 128), F32) for _ in range(4)]
-        vocab = vbuf.shape[1]
         for low in range(0, vocab, 512):
             high = min(low + 512, vocab)
             logits = jnp.dot(normed, vbuf[:, low:high], preferred_element_type=F32)
@@ -388,16 +415,8 @@
     for k in range(chips - 1):
         for i in range(chunks):
             sums(i, k)
-        if k == 0:
-            for n in range(1, shards):
-                w_mp(n).start()
     for i in range(chunks):
         attended(i)
-    for n in range(1, shards):
-        w_mp(n).wait_recv()
-    own_w.wait()
-    for n in range(1, groups):
-        w_dp(n, grp).start()
     for k in range(1, chips):
         for i in range(chunks):
             first[i].forward(k)
@@ -434,9 +453,12 @@
             total_copy(i, n).wait_send()
 
 
-def hidden_of(shards, groups, part, out_weight, res, gain, marks, vocab_weight):
-    own, width = part.shape[1], out_weight.shape[1]
-    wide = part.shape[2]
+def hidden_of(
+    shards, groups, lengths, queries, cache_keys, cache_values, new_keys, new_values, parents,
+    tree_tokens, residual, out_weight, gain, vocab_weight,
+):
+    own, width = queries.shape[1:]
+    wide = width + 128
     ncol = width // shards
     chips = shards // 2
     chunks = own // CHUNK
@@ -446,14 +468,25 @@
     vmem = pl.BlockSpec(memory_space=pltpu.VMEM)
     return pl.pallas_call(
         functools.partial(hidden_kernel, chips, groups),
-        in_specs=[anywhere, vmem, vmem, vmem, vmem, anywhere],
+        in_specs=[pl.BlockSpec(memory_space=pltpu.SMEM)] + [anywhere] * 8 + [vmem, vmem, anywhere],
         out_specs=[vmem, vmem],
         out_shape=[
             jax.ShapeDtypeStruct((shards, own, width), BF16),
             jax.ShapeDtypeStruct((chunks, 8, shards * CHUNK), F32),
         ],
         scratch_shapes=[
-            pltpu.VMEM((chips, own, wide), BF16),
+            pltpu.VMEM(queries.shape, BF16),
+            pltpu.VMEM(cache_keys.shape, BF16),
+            pltpu.VMEM(cache_values.shape, BF16),
+            pltpu.VMEM(new_keys.shape, BF16),
+            pltpu.VMEM(new_values.shape, BF16),
+            pltpu.VMEM(parents.shape, jnp.int32),
+            pltpu.VMEM(tree_tokens.shape, jnp.int32),
+            pltpu.VMEM((shards, own, ncol), BF16),
+            pltpu.VMEM((own, shards, 128), F32),
+            pltpu.VMEM((128, 128), F32),
+            pltpu.VMEM((shards, own, wide), BF16),
+            dma((shards,)), dma((shards,)), dma((shards,)), dma, dma, dma,
             pltpu.VMEM((chips, own, wide), BF16),
             pltpu.VMEM((chips, own, wide), BF16),
             pltpu.VMEM((chips, own, wide), BF16),
@@ -462,7 +495,7 @@
             pltpu.VMEM((shards, own, width), BF16),
             pltpu.VMEM((groups, shards, out_weight.shape[0], ncol), BF16),
             pltpu.VMEM((shards, chunks, shards * CHUNK, ncol), BF16),
-            *[dma((chunks, chips))] * 6,
+            *[dma((chunks, chips))] * 5,
             *gather_sems,
             *gather_sems,
             dma((shards,)), dma((shards,)), dma((groups,)), dma((groups,)), dma,
@@ -475,7 +508,10 @@
             collective_id=0, has_side_effects=True, vmem_limit_bytes=VMEM_LIMIT
         ),
         name="hidden_exchange",
-    )(part, out_weight, res, gain, marks, vocab_weight)
+    )(
+        lengths, queries, cache_keys, cache_values, new_keys, new_values, parents, tree_tokens,
+        residual, out_weight, gain, vocab_weight,
+    )
 
 
 def local_fast(
@@ -484,34 +520,14 @@
 ):
     reqs, tree, width = queries.shape
     tokens = reqs * tree
-    shard = lax.axis_index("mp")
     shards = lax.axis_size("mp")
     groups = lax.axis_size("dp")
-    ncol = width // shards
-    part = attention(
-        shards, queries, new_keys, new_values, cache_keys, cache_values, lengths, parents
-    ).reshape(shards, tokens // shards, width + 128)
-    res = lax.dynamic_slice_in_dim(residual.reshape(tokens, width), shard * ncol, ncol, 1)
-    res = res.reshape(shards, tokens // shards, ncol)
-    vocab = vocab_weight.shape[1]
-    column = tree_tokens - shard * vocab
-    column = jnp.where((column >= 0) & (column < vocab), column, -1)
     idx = jnp.arange(tree, dtype=jnp.int32)[None, :]
     by_one = (parents == idx - 1) & (idx > 0)
-    by_two = (parents == idx - 2) & (idx > 1)
-
-    def ahead(x, n):
-        return jnp.pad(x[:, n:], ((0, 0), (0, n)), constant_values=-1)
-
-    first = jnp.where(idx == 0, column, -1)
-    marks = jnp.stack(
-        [ahead(jnp.where(by_one, column, -1), 1), ahead(jnp.where(by_two, column, -1), 2), first], -1
-    ).reshape(tokens, 3)
-    marks = jnp.pad(marks, ((0, 0), (0, 125)), constant_values=-1)
     own = tokens // shards
     hidden, stats = hidden_of(
-        shards, groups, part, out_weight, res, norm_gain.reshape(1, width),
-        marks.reshape(shards, own, 128), vocab_weight,
+        shards, groups, lengths, queries, cache_keys, cache_values, new_keys, new_values, parents,
+        tree_tokens, residual, out_weight, norm_gain.reshape(1, width), vocab_weight,
     )
     total = stats.reshape(own // CHUNK, 8, shards, CHUNK).transpose(1, 2, 0, 3)
     total = total.reshape(8, reqs, tree)
@@ -614,7 +630,8 @@
         and tree % 16 == 0
         and vocab_weight.shape[1] % 128 == 0
         and shards % 2 == 0
-        and shards >= 8
+        and shards == 8
+        and reqs == shards
     )
     return (local_fast if fits else local_plain)(*args)
 

time: 99.2 us -> 88.2 us (0.89)
  Pallas kernels: 89.5 us -> 82.7 us
  local copies, waits for them, and re-layouts: 7.26 us -> 3.92 us
    pallas_call x1 -> x0, Pallas kernels: 9.92 us -> none  [attention(): pl.pallas_call(functools.partial(attention_kernel, shards), grid=(reqs,),...]
    pallas_call x1, Pallas kernels: 79.6 us -> 82.7 us  [hidden_of(): pl.pallas_call(functools.partial(hidden_kernel, chips, groups), in_specs=...]
    unnamed x4 -> x3, local copies, waits for them, and re-layouts: 4.27 us -> 2.73 us
where the time goes in v5:
time: 88.2 us; the launch traced here: 88 us
  Pallas kernels  82.7 us (94%)
  local copies, waits for them, and re-layouts  3.92 us (4%)
    pallas_call x1, Pallas kernels, hidden_of(): pl.pallas_call(functools.partial(hidden_kernel, chips, groups), in_specs=...  82.7 us
    unnamed x3, local copies, waits for them, and re-layouts  2.73 us

profile of v5, /device:TPU:0, one launch (start us, length us, event | category | flops | bytes accessed | tf_op | source)
XLA Modules:
  0.0 88.0 jit_solution(3828955104467327826)
XLA Ops:
  0.6 0.0 copy-start
  0.6 82.7 %hidden_exchange.1 = (bf16[8,48,2048]{2,1,0:T(8,128)(2,1)}, f32[3,8,128]{2,1,0:T(8,128)}) custom-call(s32[8]{0:T(128)} %len_ref.1, bf16[8,48,2048]{2,1,0:T(8,128)(2,1)} %q_hbm.1, bf16[8,128,2048]{2,1,0:T(8,128)(2,1)} %k_hbm.1, bf16[8,128,2048]{2,1,0:T(8,128)(2,1)} %v_hbm.1, bf16[8,48,2048]{2,1,0:T(8,128)(2,1)} %nk_hbm.1, bf16[8,48,2048]{2,1,0:T(8,128)(2,1)} %nv_hbm.1, ...), custom_call_target="tpu_custom_call" | custom-call | tf_op jit(solution)/shard_map/hidden_exchange/pallas_call | solution.py:469
  83.3 0.8 reshape.35
  84.1 0.1 copy.20
  84.2 0.1 squeeze.15
  84.3 0.1 squeeze.14
  84.4 0.1 squeeze.13
  84.5 0.1 squeeze.12
  84.6 0.0 copy-done
  84.6 0.7 log_subtract_fusion
  85.2 2.7 %copy.22 = bf16[8,48,2048]{2,1,0:T(8,128)(2,1)} copy(bf16[8,48,2048]{2,1,0:T(8,128)(2,1)} %get-tuple-element.14) | data formatting | bytes 3145728
  (3 shorter events, 0.0 us)
Async XLA Ops:
  0.6 83.9 %copy-start = (s32[8,48]{1,0:T(8,128)S(1)}, s32[8,48]{1,0:T(8,128)}, u32[]{:S(2)}) copy-start(s32[8,48]{1,0:T(8,128)} %par_hbm.1) | copy-start | bytes 4612

commit v6 on v5

--- a/solution.py
+++ b/solution.py
@@ -412,25 +412,25 @@
                     j, i, t * CHUNK : (t + 1) * CHUNK
                 ]
 
-    for k in range(chips - 1):
-        for i in range(chunks):
-            sums(i, k)
-    for i in range(chunks):
-        attended(i)
-    for k in range(1, chips):
-        for i in range(chunks):
-            first[i].forward(k)
-    for i in range(chunks):
-        project(i)
-    for k in range(1, chips - 1):
-        for i in range(chunks):
-            second[i].forward(k)
-    for i in range(chunks):
+    def finish_hidden(i):
         second[i].forward(chips - 1)
         place(i)
+
+    def finish_scores(i):
         if i == 0:
             load_vocab.wait()
         score(i)
+
+    stages = [lambda i, k=k: sums(i, k) for k in range(chips - 1)]
+    stages += [attended]
+    stages += [lambda i, k=k: first[i].forward(k) for k in range(1, chips)]
+    stages += [project]
+    stages += [lambda i, k=k: second[i].forward(k) for k in range(1, chips - 1)]
+    stages += [finish_hidden, finish_scores]
+    for turn in range(len(stages) + chunks - 1):
+        live = [i for i in range(chunks) if 0 <= turn - i < len(stages)]
+        for i in sorted(live, key=lambda i: stages[turn - i] is finish_scores):
+            stages[turn - i](i)
     for i in range(chunks):
         total = stats[i]
         for n in range(1, shards):

time: 88.2 us -> 90.4 us (1.025)
  Pallas kernels: 82.7 us -> 84.9 us
    pallas_call x1, Pallas kernels: 82.7 us -> 84.9 us  [hidden_of(): pl.pallas_call(functools.partial(hidden_kernel, chips, groups), in_specs=...]
where the time goes in v6:
time: 90.4 us; the launch traced here: 90.2 us
  Pallas kernels  84.9 us (94%)
  local copies, waits for them, and re-layouts  3.92 us (4%)
    pallas_call x1, Pallas kernels, hidden_of(): pl.pallas_call(functools.partial(hidden_kernel, chips, groups), in_specs=...  84.9 us
    unnamed x3, local copies, waits for them, and re-layouts  2.73 us

profile of v6, /device:TPU:0, one launch (start us, length us, event | category | flops | bytes accessed | tf_op | source)
XLA Modules:
  0.0 90.2 jit_solution(8614769912228107012)
XLA Ops:
  0.6 0.0 copy-start
  0.6 84.9 %hidden_exchange.1 = (bf16[8,48,2048]{2,1,0:T(8,128)(2,1)}, f32[3,8,128]{2,1,0:T(8,128)}) custom-call(s32[8]{0:T(128)} %len_ref.1, bf16[8,48,2048]{2,1,0:T(8,128)(2,1)} %q_hbm.1, bf16[8,128,2048]{2,1,0:T(8,128)(2,1)} %k_hbm.1, bf16[8,128,2048]{2,1,0:T(8,128)(2,1)} %v_hbm.1, bf16[8,48,2048]{2,1,0:T(8,128)(2,1)} %nk_hbm.1, bf16[8,48,2048]{2,1,0:T(8,128)(2,1)} %nv_hbm.1, ...), custom_call_target="tpu_custom_call" | custom-call | tf_op jit(solution)/shard_map/hidden_exchange/pallas_call | solution.py:469
  85.5 0.8 reshape.35
  86.3 0.1 copy.20
  86.4 0.1 squeeze.15
  86.5 0.1 squeeze.14
  86.6 0.1 squeeze.13
  86.7 0.1 squeeze.12
  86.8 0.0 copy-done
  86.8 0.7 log_subtract_fusion
  87.4 2.7 %copy.22 = bf16[8,48,2048]{2,1,0:T(8,128)(2,1)} copy(bf16[8,48,2048]{2,1,0:T(8,128)(2,1)} %get-tuple-element.14) | data formatting | bytes 3145728
  (3 shorter events, 0.0 us)
Async XLA Ops:
  0.6 86.1 %copy-start = (s32[8,48]{1,0:T(8,128)S(1)}, s32[8,48]{1,0:T(8,128)}, u32[]{:S(2)}) copy-start(s32[8,48]{1,0:T(8,128)} %par_hbm.1) | copy-start | bytes 4612
